TPU v7x, 256 devices: a whole 4x4x8 slice. The times are simulated.
256 devices in a mesh: slab: 8 (over y, core), tile: 32 (over x, z).
Axes of the slice: x: 4, y: 4, z: 8, core: 2. Of those that a mesh axis runs over, the one named last changes fastest.
Arguments:
- local_field: float32 [2, 64, 8, 49152], P(None, None, 'slab', 'tile'), may hold values from -6 to 6
- material: int32 [8, 49152], P('slab', 'tile'), may hold values from 0 to 15
- contrast: float32 [16], replicated, may hold values from 0.5 to 1.2
- low_left: float32 [8, 2, 256, 49152], P('slab', None, None, 'tile'), may hold values from -0.21875 to 0.21875
- low_right: float32 [8, 2, 49152, 256], P('slab', None, 'tile'), may hold values from -0.02734375 to 0.02734375
- near_blocks: float32 [8, 2, 384, 384, 128], P('slab', None, 'tile'), may hold values from -0.21875 to 0.21875
Outputs:
- traces: float32 [2, 64, 8, 49152], P(None, None, 'slab', 'tile')
All inputs are finite; a program needn't handle non-finite values.
Results may differ from a plain program's by a relative error of at most 0.00014.
Values sent between devices are 32-bit elements; how exact they have to be, the bound alone decides.
No kernel may reach another device: no remote copies, remote signals or barrier semaphores. Data moves between devices by JAX's collectives and lax.ppermute only.
A program may use at most 64 MiB of HBM per device.

v0:
```python
import jax
import jax.numpy as jnp
from jax import lax
from jax.sharding import PartitionSpec as P


def with_halo(shard, sides, width):
    for axis, dim in sides:
        size, length = (lax.axis_size(axis), shard.shape[dim])
        up = [(i, (i + 1) % size) for i in range(size - 1)]
        down = [(j, i) for i, j in up]
        last = lax.slice_in_dim(shard, length - width, length, axis=dim)
        initial = lax.slice_in_dim(shard, 0, width, axis=dim)
        before = lax.ppermute(last, axis, up)
        after = lax.ppermute(initial, axis, down)
        shard = jnp.concatenate([before, shard, after], axis=dim)
    return shard


def passed_along(block, axis, distance):
    devices = range(lax.axis_size(axis))
    route = [(i - distance, i) for i in devices if i - distance in devices]
    return lax.ppermute(block, axis, route)


def complex_product(pattern, first, second):
    high = lax.Precision.HIGHEST
    real_part = jnp.einsum(pattern, first[0], second[0], precision=high) - jnp.einsum(
        pattern, first[1], second[1], precision=high
    )
    imag_part = jnp.einsum(pattern, first[0], second[1], precision=high) + jnp.einsum(
        pattern, first[1], second[0], precision=high
    )
    return jnp.stack([real_part, imag_part])


def near_product(extended, blocks, points):
    block_width = blocks.shape[-1]
    block_count = points // block_width
    sources = extended.shape[1]
    pieces = [
        extended[:, :, k * block_width : k * block_width + points].reshape(
            2, sources, block_count, block_width
        )
        for k in range(3)
    ]
    windows = jnp.concatenate(pieces, axis=-1)
    return complex_product("sbk,bki->sbi", windows, blocks).reshape(2, sources, points)


def rim_product(incoming, near_local):
    block_width = near_local.shape[-1]
    extended = with_halo(incoming, (("tile", 2),), block_width)
    return near_product(extended, near_local, incoming.shape[2])


def total_coefficients(partial_sums):
    return lax.psum(partial_sums, "tile")


def pass_downward(outgoing):
    return passed_along(outgoing, "slab", 1)


def on_device(local_field, material, contrast, low_left, low_right, near_blocks):
    source_field = local_field[:, :, 0]
    left_factor = low_left[0]
    right_factor = low_right[0]
    near_local = near_blocks[0]
    points = source_field.shape[2]
    sources = source_field.shape[1]
    onehot_table = (
        material[0][:, None] == jnp.arange(contrast.shape[0], dtype=jnp.int32)[None, :]
    ).astype(jnp.float32)
    contrast_at = jnp.dot(onehot_table, contrast, precision=lax.Precision.HIGHEST)

    def apply_kernel(incoming):
        partial_sums = complex_product("sp,pr->sr", incoming, right_factor)
        coefficients = total_coefficients(partial_sums)
        close_part = rim_product(incoming, near_local)
        far_part = complex_product("sr,rp->sp", coefficients, left_factor)
        return far_part + close_part

    slab_count = lax.axis_size("slab")

    def advance_whole(step_index, outgoing):
        received = pass_downward(outgoing)
        return source_field + contrast_at * apply_kernel(received)

    result = lax.fori_loop(
        0, slab_count, advance_whole, jnp.zeros((2, sources, points), jnp.float32)
    )
    return result[:, :, None, :]


def solution(mesh):
    return jax.shard_map(
        on_device,
        mesh=mesh,
        in_specs=(
            P(None, None, "slab", "tile"),
            P("slab", "tile"),
            P(),
            P("slab", None, None, "tile"),
            P("slab", None, "tile", None),
            P("slab", None, "tile", None, None),
        ),
        out_specs=P(None, None, "slab", "tile"),
        check_vma=False,
    )
```

profile of v0, /device:TPU:1, one launch (start us, length us, event | category | flops | bytes accessed | tf_op | source)
XLA Modules:
  0.0 1400.2 jit_solution(9820627663527672870)
XLA Ops:
  9.9 1382.0 %while.11 = (s32[]{:T(128)}, f32[2,64,1536]{2,1,0:T(8,128)S(1)}, f32[1536]{0:T(1024)S(1)}, f32[2,1536,256]{2,1,0:T(8,128)}, f32[2,256,1536]{2,1,0:T(8,128)}, /*i...) while((s32[]{:T(128)}, f32[2,64,1536]{2,1,0:T(8,128)S(1)}, ...), condition=%wide.region_2.0_spmd.clone, body=%wide.region_0.0_spmd.clone.sunk | while | flops 4229922816 | bytes 98310584 | solution.py:90
  10.1 4.6 collective-permute-start
  14.7 8.9 collective-permute-done
  24.9 4.2 collective-permute-start.2
  36.7 3.6 fusion.121
  43.9 2.6 fusion.120
  52.6 125.5 %all-reduce.2.cloned.1.call-done = f32[2,64,256]{2,1,0:T(8,128)} async-done(((f32[2,64,256]{2,1,0:T(8,128)}), f32[2,64,256]{2,1,0:T(8,128)}) %all-reduce.2.cloned.1.call-update) | async-done | bytes 131088 | tf_op jit(solution)/shard_map/while/body/eval_jaxpr/psum | solution.py:58
  184.5 7.4 collective-permute-start
  192.0 8.9 collective-permute-done
  202.2 4.0 collective-permute-start.2
  213.8 3.6 fusion.121
  221.0 2.6 fusion.120
  229.7 120.9 %all-reduce.2.cloned.1.call-done = f32[2,64,256]{2,1,0:T(8,128)} async-done(((f32[2,64,256]{2,1,0:T(8,128)}), f32[2,64,256]{2,1,0:T(8,128)}) %all-reduce.2.cloned.1.call-update) | async-done | bytes 131088 | tf_op jit(solution)/shard_map/while/body/eval_jaxpr/psum | solution.py:58
  357.0 7.4 collective-permute-start
  364.5 8.9 collective-permute-done
  374.7 4.0 collective-permute-start.2
  386.3 3.6 fusion.121
  393.5 2.6 fusion.120
  402.2 121.0 %all-reduce.2.cloned.1.call-done = f32[2,64,256]{2,1,0:T(8,128)} async-done(((f32[2,64,256]{2,1,0:T(8,128)}), f32[2,64,256]{2,1,0:T(8,128)}) %all-reduce.2.cloned.1.call-update) | async-done | bytes 131088 | tf_op jit(solution)/shard_map/while/body/eval_jaxpr/psum | solution.py:58
  529.6 7.4 collective-permute-start
  537.0 8.9 collective-permute-done
  547.2 4.0 collective-permute-start.2
  558.8 3.6 fusion.121
  566.1 2.6 fusion.120
  574.8 120.9 %all-reduce.2.cloned.1.call-done = f32[2,64,256]{2,1,0:T(8,128)} async-done(((f32[2,64,256]{2,1,0:T(8,128)}), f32[2,64,256]{2,1,0:T(8,128)}) %all-reduce.2.cloned.1.call-update) | async-done | bytes 131088 | tf_op jit(solution)/shard_map/while/body/eval_jaxpr/psum | solution.py:58
  702.0 7.4 collective-permute-start
  709.5 8.9 collective-permute-done
  719.7 4.0 collective-permute-start.2
  731.3 3.6 fusion.121
  738.5 2.6 fusion.120
  747.2 121.0 %all-reduce.2.cloned.1.call-done = f32[2,64,256]{2,1,0:T(8,128)} async-done(((f32[2,64,256]{2,1,0:T(8,128)}), f32[2,64,256]{2,1,0:T(8,128)}) %all-reduce.2.cloned.1.call-update) | async-done | bytes 131088 | tf_op jit(solution)/shard_map/while/body/eval_jaxpr/psum | solution.py:58
  874.6 7.4 collective-permute-start
  882.0 8.9 collective-permute-done
  892.2 4.0 collective-permute-start.2
  903.8 3.6 fusion.121
  911.1 2.6 fusion.120
  919.8 120.9 %all-reduce.2.cloned.1.call-done = f32[2,64,256]{2,1,0:T(8,128)} async-done(((f32[2,64,256]{2,1,0:T(8,128)}), f32[2,64,256]{2,1,0:T(8,128)}) %all-reduce.2.cloned.1.call-update) | async-done | bytes 131088 | tf_op jit(solution)/shard_map/while/body/eval_jaxpr/psum | solution.py:58
  1047.1 7.4 collective-permute-start
  1054.5 8.9 collective-permute-done
  1064.7 4.0 collective-permute-start.2
  1076.3 3.6 fusion.121
  1083.6 2.6 fusion.120
  1092.3 121.0 %all-reduce.2.cloned.1.call-done = f32[2,64,256]{2,1,0:T(8,128)} async-done(((f32[2,64,256]{2,1,0:T(8,128)}), f32[2,64,256]{2,1,0:T(8,128)}) %all-reduce.2.cloned.1.call-update) | async-done | bytes 131088 | tf_op jit(solution)/shard_map/while/body/eval_jaxpr/psum | solution.py:58
  1219.6 7.4 collective-permute-start
  1227.1 8.9 collective-permute-done
  1237.3 4.0 collective-permute-start.2
  1248.9 3.6 fusion.121
  1264.8 120.9 %all-reduce.2.cloned.1.call-done = f32[2,64,256]{2,1,0:T(8,128)} async-done(((f32[2,64,256]{2,1,0:T(8,128)}), f32[2,64,256]{2,1,0:T(8,128)}) %all-reduce.2.cloned.1.call-update) | async-done | bytes 131088 | tf_op jit(solution)/shard_map/while/body/eval_jaxpr/psum | solution.py:58
  (344 shorter events, 206.5 us)
Async XLA Ops:
  10.0 168.2 %all-reduce.2.cloned.1.call-start = ((), (), s32[]{:S(2)}) async-start(), calls=%async_computation | async-start | bytes 262144 | tf_op jit(solution)/shard_map/while/body/eval_jaxpr/psum | solution.py:58
  10.1 13.5 collective-permute-start
  14.7 19.0 %copy-start.1 = (f32[2,1536,256]{2,1,0:T(8,128)S(1)}, f32[2,1536,256]{2,1,0:T(8,128)}, u32[]{:S(2)}) copy-start(f32[2,1536,256]{2,1,0:T(8,128)} %get-tuple-element.157) | copy-start | bytes 9437188 | tf_op jit(solution)/shard_map/while
  23.6 12.6 collective-permute-start.1
  24.9 11.4 collective-permute-start.2
  46.5 131.6 %copy-start.2 = (f32[2,256,1536]{2,1,0:T(8,128)S(1)}, f32[2,256,1536]{2,1,0:T(8,128)}, u32[]{:S(2)}) copy-start(f32[2,256,1536]{2,1,0:T(8,128)} %get-tuple-element.158) | copy-start | bytes 9437188 | tf_op jit(solution)/shard_map/while
  184.4 166.2 %all-reduce.2.cloned.1.call-start = ((), (), s32[]{:S(2)}) async-start(), calls=%async_computation | async-start | bytes 262144 | tf_op jit(solution)/shard_map/while/body/eval_jaxpr/psum | solution.py:58
  184.5 16.3 %collective-permute-start = (f32[2,64,1536]{2,1,0:T(8,128)S(1)}, f32[2,64,1536]{2,1,0:T(8,128)S(1)}, u32[]{:S(2)}, u32[]{:S(2)}) collective-permute-start(f32[2,64,1536]{2,1,0:T(8,128)S(1)} %broadcast_select_fusion.2), channel_id=1, source_target_pairs={{0,32},{32,64},{64,96},{96,128},{128,160},{160,192},{192,224},{1,3... | collective-permute-start | bytes 2359304 | tf_op jit(solution)/shard_map/while/body/eval_jaxpr/ppermute | solution.py:23
  192.0 18.9 %copy-start.1 = (f32[2,1536,256]{2,1,0:T(8,128)S(1)}, f32[2,1536,256]{2,1,0:T(8,128)}, u32[]{:S(2)}) copy-start(f32[2,1536,256]{2,1,0:T(8,128)} %get-tuple-element.157) | copy-start | bytes 9437188 | tf_op jit(solution)/shard_map/while
  200.9 12.5 collective-permute-start.1
  202.2 11.2 collective-permute-start.2
  223.6 127.1 %copy-start.2 = (f32[2,256,1536]{2,1,0:T(8,128)S(1)}, f32[2,256,1536]{2,1,0:T(8,128)}, u32[]{:S(2)}) copy-start(f32[2,256,1536]{2,1,0:T(8,128)} %get-tuple-element.158) | copy-start | bytes 9437188 | tf_op jit(solution)/shard_map/while
  356.9 166.3 %all-reduce.2.cloned.1.call-start = ((), (), s32[]{:S(2)}) async-start(), calls=%async_computation | async-start | bytes 262144 | tf_op jit(solution)/shard_map/while/body/eval_jaxpr/psum | solution.py:58
  357.0 16.3 %collective-permute-start = (f32[2,64,1536]{2,1,0:T(8,128)S(1)}, f32[2,64,1536]{2,1,0:T(8,128)S(1)}, u32[]{:S(2)}, u32[]{:S(2)}) collective-permute-start(f32[2,64,1536]{2,1,0:T(8,128)S(1)} %broadcast_select_fusion.2), channel_id=1, source_target_pairs={{0,32},{32,64},{64,96},{96,128},{128,160},{160,192},{192,224},{1,3... | collective-permute-start | bytes 2359304 | tf_op jit(solution)/shard_map/while/body/eval_jaxpr/ppermute | solution.py:23
  364.5 18.9 %copy-start.1 = (f32[2,1536,256]{2,1,0:T(8,128)S(1)}, f32[2,1536,256]{2,1,0:T(8,128)}, u32[]{:S(2)}) copy-start(f32[2,1536,256]{2,1,0:T(8,128)} %get-tuple-element.157) | copy-start | bytes 9437188 | tf_op jit(solution)/shard_map/while
  373.4 12.5 collective-permute-start.1
  374.7 11.2 collective-permute-start.2
  396.1 127.1 %copy-start.2 = (f32[2,256,1536]{2,1,0:T(8,128)S(1)}, f32[2,256,1536]{2,1,0:T(8,128)}, u32[]{:S(2)}) copy-start(f32[2,256,1536]{2,1,0:T(8,128)} %get-tuple-element.158) | copy-start | bytes 9437188 | tf_op jit(solution)/shard_map/while
  529.5 166.2 %all-reduce.2.cloned.1.call-start = ((), (), s32[]{:S(2)}) async-start(), calls=%async_computation | async-start | bytes 262144 | tf_op jit(solution)/shard_map/while/body/eval_jaxpr/psum | solution.py:58
  529.6 16.3 %collective-permute-start = (f32[2,64,1536]{2,1,0:T(8,128)S(1)}, f32[2,64,1536]{2,1,0:T(8,128)S(1)}, u32[]{:S(2)}, u32[]{:S(2)}) collective-permute-start(f32[2,64,1536]{2,1,0:T(8,128)S(1)} %broadcast_select_fusion.2), channel_id=1, source_target_pairs={{0,32},{32,64},{64,96},{96,128},{128,160},{160,192},{192,224},{1,3... | collective-permute-start | bytes 2359304 | tf_op jit(solution)/shard_map/while/body/eval_jaxpr/ppermute | solution.py:23
  537.0 18.9 %copy-start.1 = (f32[2,1536,256]{2,1,0:T(8,128)S(1)}, f32[2,1536,256]{2,1,0:T(8,128)}, u32[]{:S(2)}) copy-start(f32[2,1536,256]{2,1,0:T(8,128)} %get-tuple-element.157) | copy-start | bytes 9437188 | tf_op jit(solution)/shard_map/while
  545.9 12.5 collective-permute-start.1
  547.2 11.2 collective-permute-start.2
  568.6 127.0 %copy-start.2 = (f32[2,256,1536]{2,1,0:T(8,128)S(1)}, f32[2,256,1536]{2,1,0:T(8,128)}, u32[]{:S(2)}) copy-start(f32[2,256,1536]{2,1,0:T(8,128)} %get-tuple-element.158) | copy-start | bytes 9437188 | tf_op jit(solution)/shard_map/while
  701.9 166.3 %all-reduce.2.cloned.1.call-start = ((), (), s32[]{:S(2)}) async-start(), calls=%async_computation | async-start | bytes 262144 | tf_op jit(solution)/shard_map/while/body/eval_jaxpr/psum | solution.py:58
  702.0 16.3 %collective-permute-start = (f32[2,64,1536]{2,1,0:T(8,128)S(1)}, f32[2,64,1536]{2,1,0:T(8,128)S(1)}, u32[]{:S(2)}, u32[]{:S(2)}) collective-permute-start(f32[2,64,1536]{2,1,0:T(8,128)S(1)} %broadcast_select_fusion.2), channel_id=1, source_target_pairs={{0,32},{32,64},{64,96},{96,128},{128,160},{160,192},{192,224},{1,3... | collective-permute-start | bytes 2359304 | tf_op jit(solution)/shard_map/while/body/eval_jaxpr/ppermute | solution.py:23
  709.5 18.9 %copy-start.1 = (f32[2,1536,256]{2,1,0:T(8,128)S(1)}, f32[2,1536,256]{2,1,0:T(8,128)}, u32[]{:S(2)}) copy-start(f32[2,1536,256]{2,1,0:T(8,128)} %get-tuple-element.157) | copy-start | bytes 9437188 | tf_op jit(solution)/shard_map/while
  718.4 12.5 collective-permute-start.1
  719.7 11.2 collective-permute-start.2
  741.1 127.1 %copy-start.2 = (f32[2,256,1536]{2,1,0:T(8,128)S(1)}, f32[2,256,1536]{2,1,0:T(8,128)}, u32[]{:S(2)}) copy-start(f32[2,256,1536]{2,1,0:T(8,128)} %get-tuple-element.158) | copy-start | bytes 9437188 | tf_op jit(solution)/shard_map/while
  874.5 166.2 %all-reduce.2.cloned.1.call-start = ((), (), s32[]{:S(2)}) async-start(), calls=%async_computation | async-start | bytes 262144 | tf_op jit(solution)/shard_map/while/body/eval_jaxpr/psum | solution.py:58
  874.6 16.3 %collective-permute-start = (f32[2,64,1536]{2,1,0:T(8,128)S(1)}, f32[2,64,1536]{2,1,0:T(8,128)S(1)}, u32[]{:S(2)}, u32[]{:S(2)}) collective-permute-start(f32[2,64,1536]{2,1,0:T(8,128)S(1)} %broadcast_select_fusion.2), channel_id=1, source_target_pairs={{0,32},{32,64},{64,96},{96,128},{128,160},{160,192},{192,224},{1,3... | collective-permute-start | bytes 2359304 | tf_op jit(solution)/shard_map/while/body/eval_jaxpr/ppermute | solution.py:23
  882.0 18.9 %copy-start.1 = (f32[2,1536,256]{2,1,0:T(8,128)S(1)}, f32[2,1536,256]{2,1,0:T(8,128)}, u32[]{:S(2)}) copy-start(f32[2,1536,256]{2,1,0:T(8,128)} %get-tuple-element.157) | copy-start | bytes 9437188 | tf_op jit(solution)/shard_map/while
  890.9 12.5 collective-permute-start.1
  892.2 11.2 collective-permute-start.2
  913.7 127.0 %copy-start.2 = (f32[2,256,1536]{2,1,0:T(8,128)S(1)}, f32[2,256,1536]{2,1,0:T(8,128)}, u32[]{:S(2)}) copy-start(f32[2,256,1536]{2,1,0:T(8,128)} %get-tuple-element.158) | copy-start | bytes 9437188 | tf_op jit(solution)/shard_map/while
  1046.9 166.3 %all-reduce.2.cloned.1.call-start = ((), (), s32[]{:S(2)}) async-start(), calls=%async_computation | async-start | bytes 262144 | tf_op jit(solution)/shard_map/while/body/eval_jaxpr/psum | solution.py:58
  1047.1 16.3 %collective-permute-start = (f32[2,64,1536]{2,1,0:T(8,128)S(1)}, f32[2,64,1536]{2,1,0:T(8,128)S(1)}, u32[]{:S(2)}, u32[]{:S(2)}) collective-permute-start(f32[2,64,1536]{2,1,0:T(8,128)S(1)} %broadcast_select_fusion.2), channel_id=1, source_target_pairs={{0,32},{32,64},{64,96},{96,128},{128,160},{160,192},{192,224},{1,3... | collective-permute-start | bytes 2359304 | tf_op jit(solution)/shard_map/while/body/eval_jaxpr/ppermute | solution.py:23
  1054.5 18.9 %copy-start.1 = (f32[2,1536,256]{2,1,0:T(8,128)S(1)}, f32[2,1536,256]{2,1,0:T(8,128)}, u32[]{:S(2)}) copy-start(f32[2,1536,256]{2,1,0:T(8,128)} %get-tuple-element.157) | copy-start | bytes 9437188 | tf_op jit(solution)/shard_map/while
  1063.4 12.5 collective-permute-start.1
  1064.7 11.2 collective-permute-start.2
  1086.1 127.1 %copy-start.2 = (f32[2,256,1536]{2,1,0:T(8,128)S(1)}, f32[2,256,1536]{2,1,0:T(8,128)}, u32[]{:S(2)}) copy-start(f32[2,256,1536]{2,1,0:T(8,128)} %get-tuple-element.158) | copy-start | bytes 9437188 | tf_op jit(solution)/shard_map/while
  1219.5 166.2 %all-reduce.2.cloned.1.call-start = ((), (), s32[]{:S(2)}) async-start(), calls=%async_computation | async-start | bytes 262144 | tf_op jit(solution)/shard_map/while/body/eval_jaxpr/psum | solution.py:58
  1219.6 16.3 %collective-permute-start = (f32[2,64,1536]{2,1,0:T(8,128)S(1)}, f32[2,64,1536]{2,1,0:T(8,128)S(1)}, u32[]{:S(2)}, u32[]{:S(2)}) collective-permute-start(f32[2,64,1536]{2,1,0:T(8,128)S(1)} %broadcast_select_fusion.2), channel_id=1, source_target_pairs={{0,32},{32,64},{64,96},{96,128},{128,160},{160,192},{192,224},{1,3... | collective-permute-start | bytes 2359304 | tf_op jit(solution)/shard_map/while/body/eval_jaxpr/ppermute | solution.py:23
  1227.0 18.9 %copy-start.1 = (f32[2,1536,256]{2,1,0:T(8,128)S(1)}, f32[2,1536,256]{2,1,0:T(8,128)}, u32[]{:S(2)}) copy-start(f32[2,1536,256]{2,1,0:T(8,128)} %get-tuple-element.157) | copy-start | bytes 9437188 | tf_op jit(solution)/shard_map/while
  1236.0 12.5 collective-permute-start.1
  1237.3 11.2 collective-permute-start.2
  1258.7 127.0 %copy-start.2 = (f32[2,256,1536]{2,1,0:T(8,128)S(1)}, f32[2,256,1536]{2,1,0:T(8,128)}, u32[]{:S(2)}) copy-start(f32[2,256,1536]{2,1,0:T(8,128)} %get-tuple-element.158) | copy-start | bytes 9437188 | tf_op jit(solution)/shard_map/while
  (41 other events, 151.9 us)
Sparse Core Ops, SparseCore 0:
  36.4 141.7 all-reduce.1
  213.5 137.1 all-reduce.1
  386.0 137.1 all-reduce.1
  558.5 137.1 all-reduce.1
  731.0 137.1 all-reduce.1
  903.5 137.1 all-reduce.1
  1076.0 137.1 all-reduce.1
  1248.6 137.1 all-reduce.1
where the time goes:
time: 1410 us; the launch traced here: 1400 us
  waiting for transfers between devices  1040 us (74%)
  matrix products  178 us (13%)
  starting transfers between devices  99.3 us (7%)
  local copies, waits for them, and re-layouts  54.9 us (4%)
    psum x8, waiting for transfers between devices, total_coefficients(): return lax.psum(partial_sums, 'tile')  972 us
    ppermute x8, waiting for transfers between devices, passed_along(): return lax.ppermute(block, axis, route)  71.2 us
    ppermute x8, starting transfers between devices, passed_along(): return lax.ppermute(block, axis, route)  56.5 us
    dot_general x24, matrix products, complex_product(): jnp.einsum(pattern, first[1], second[1], precision=high)  55.7 us
    dot_general x24, matrix products, complex_product(): jnp.einsum(pattern, first[1], second[0], precision=high)  47.5 us
    dot_general x24, matrix products, complex_product(): jnp.einsum(pattern, first[0], second[0], precision=high)  37.5 us
    dot_general x24, matrix products, complex_product(): jnp.einsum(pattern, first[0], second[1], precision=high)  37 us
    ppermute x8, starting transfers between devices, with_halo(): before = lax.ppermute(last, axis, up)  32.1 us
  transfers between devices with their start and end apart: 32, of which 16 were waited for; matrix products, arithmetic and copies ran while one was open for 13% of the time, Pallas kernels for 0%

commit v1 on v0

v1 whole, which is shorter than its diff:
```python
import functools
import jax
import jax.numpy as jnp
from jax import lax
from jax.experimental import pallas as pl
from jax.experimental.pallas import tpu as pltpu
from jax.sharding import PartitionSpec as P

AXES = ("slab", "tile")
BLOCK = 128
PARAMS = pltpu.CompilerParams(vmem_limit_bytes=44 * 1024 * 1024)
SMEM = pl.BlockSpec(memory_space=pltpu.SMEM)


def halves(x):
    high = x.astype(jnp.bfloat16)
    low = (x - high.astype(jnp.float32)).astype(jnp.bfloat16)
    return high, low


def dot(a, b):
    return jnp.dot(a, b, preferred_element_type=jnp.float32)


def split_dot(high, low, w_high, w_low):
    rows = high.shape[0]
    both = dot(jnp.concatenate([high, low], axis=0), w_high)
    return both[:rows] + both[rows:] + dot(high, w_low)


def complex_dot(high, low, wr_high, wr_low, wi_high, wi_low):
    with_real = split_dot(high, low, wr_high, wr_low)
    with_imag = split_dot(high, low, wi_high, wi_low)
    half = with_real.shape[0] // 2
    return jnp.concatenate(
        [
            with_real[:half] - with_imag[half:],
            with_imag[:half] + with_real[half:],
        ],
        axis=0,
    )


def at_step(step, body):
    pl.when(pl.program_id(0) == step)(body)


def store_edges(steps, part, first_ref, last_ref):
    def store_first():
        first_ref[...] = part[:, :BLOCK]

    def store_last():
        last_ref[...] = part[:, -BLOCK:]

    at_step(0, store_first)
    at_step(steps - 1, store_last)


def right_kernel(steps, count, flags, *refs):
    xs, (rh_ref, rl_ref, p_ref, acc) = refs[:count], refs[count:]
    x = xs[0][...]
    if count == 2:
        x = jnp.where(flags[3] == 1, xs[1][...], jnp.where(flags[0] == 1, 0.0, x))
    high, low = halves(x)
    share = complex_dot(high, low, rh_ref[0], rl_ref[0], rh_ref[1], rl_ref[1])

    def start():
        acc[...] = share

    def finish():
        whole = acc[...]
        p_ref[0] = whole[:, :BLOCK].reshape(p_ref.shape[1:])
        p_ref[1] = whole[:, BLOCK:].reshape(p_ref.shape[1:])

    at_step(0, start)

    @pl.when(pl.program_id(0) > 0)
    def _():
        acc[...] += share

    at_step(steps - 1, finish)


def far_kernel(steps, count, pick, flags, *refs):
    coefs, refs = refs[:count], refs[count:]
    weights, refs = refs[: 2 * count], refs[2 * count :]
    bases, outs = (refs[:2], refs[2:]) if pick else (refs[:1], refs[1:])
    base = bases[0][...]
    if pick:
        base = jnp.where(flags[3] == 1, bases[1][...], base)
    total = base
    for k in range(count):
        c_ref, high_ref, low_ref = coefs[k], weights[2 * k], weights[2 * k + 1]
        c = jnp.concatenate([c_ref[0].reshape(-1, BLOCK), c_ref[1].reshape(-1, BLOCK)], axis=1)
        high, low = halves(c)
        more = complex_dot(high, low, high_ref[0], low_ref[0], high_ref[1], low_ref[1])
        if k == 1:
            more = jnp.where(flags[3] == 1, more, 0.0)
        total = total + more
    outs[0][...] = total
    if len(outs) > 1:
        store_edges(steps, total, *outs[1:])


def near_kernel(steps, group, own, edges, flags, x_ref, before_ref, after_ref, *refs):
    if own:
        l_ref, refs = refs[0], refs[1:]
    nh_ref, nl_ref, w_ref = refs[:3]
    high, low = refs[-2:]
    points = x_ref.shape[1]

    def load():
        before = jnp.where(flags[1] == 1, 0.0, before_ref[...])
        after = jnp.where(flags[2] == 1, 0.0, after_ref[...])
        high[:, :BLOCK], low[:, :BLOCK] = halves(before)
        high[:, BLOCK : BLOCK + points], low[:, BLOCK : BLOCK + points] = halves(x_ref[...])
        high[:, BLOCK + points :], low[:, BLOCK + points :] = halves(after)

    at_step(0, load)
    parts = []
    for k in range(group):
        start = pl.multiple_of((pl.program_id(0) * group + k) * BLOCK, BLOCK)
        window = pl.ds(start, 3 * BLOCK)
        both = split_dot(high[:, window], low[:, window], nh_ref[k], nl_ref[k])
        half = both.shape[0] // 2
        part = jnp.concatenate(
            [
                both[:half, :BLOCK] - both[half:, BLOCK:],
                both[:half, BLOCK:] + both[half:, :BLOCK],
            ],
            axis=0,
        )
        here = slice(k * BLOCK, (k + 1) * BLOCK)
        if own:
            mine = l_ref[:, here]
            part = jnp.where(flags[0] == 1, mine, mine + part)
        w_ref[:, here] = part
        parts.append(part)
    if edges:

        def store_first():
            refs[3][...] = parts[0]

        def store_last():
            refs[4][...] = parts[-1]

        at_step(0, store_first)
        at_step(steps - 1, store_last)


def scale_kernel(x_ref, factor_ref, high_ref, low_ref):
    high_ref[...], low_ref[...] = halves(x_ref[...] * factor_ref[...])


def split_kernel(x_ref, high_ref, low_ref):
    high_ref[...], low_ref[...] = halves(x_ref[...])


def pair_kernel(x_ref, factor_ref, high_ref, low_ref):
    for k in range(2):
        here = slice(k * BLOCK, (k + 1) * BLOCK)
        high_ref[:, :, here], low_ref[:, :, here] = halves(x_ref[k] * factor_ref[...])


def sum_kernel(parts_ref, copies_ref):
    copies_ref[...] = jnp.broadcast_to(jnp.sum(parts_ref[...], axis=0)[None], copies_ref.shape)


def f32(*shape):
    return jax.ShapeDtypeStruct(shape, jnp.float32)


def call(body, grid, args, ins, outs, out_shape, flops=0, scratch=()):
    size = sum(a.size * a.dtype.itemsize for a in args)
    return pl.pallas_call(
        body,
        grid=grid,
        in_specs=ins,
        out_specs=outs,
        out_shape=out_shape,
        scratch_shapes=scratch,
        compiler_params=PARAMS,
        cost_estimate=pl.CostEstimate(flops=flops, bytes_accessed=size, transcendentals=0),
    )(*args)


def fixed(*shape):
    return pl.BlockSpec(shape, lambda i: (0,) * len(shape))


def chunk_of(points):
    return 512 if points % 512 == 0 else BLOCK


def right_call(flags, xs, weights):
    rows, points = xs[0].shape
    rank = weights[0].shape[2]
    chunk = chunk_of(points)
    steps = points // chunk
    trace = pl.BlockSpec((rows, chunk), lambda i: (0, i))
    right = pl.BlockSpec((2, chunk, rank), lambda i: (0, i, 0))
    shape = (2, rows // 8, 8, BLOCK)
    return call(
        functools.partial(right_kernel, steps, len(xs)),
        (steps,),
        (flags, *xs, *weights),
        [SMEM, *[trace] * len(xs), right, right],
        fixed(*shape),
        f32(*shape),
        3 * 4 * rows * points * rank,
        [pltpu.VMEM((rows, rank), jnp.float32)],
    )


def far_call(flags, coefs, weights, bases, edges):
    rows, points = bases[0].shape
    rank = weights[0].shape[1]
    chunk = chunk_of(points)
    steps = points // chunk
    trace = pl.BlockSpec((rows, chunk), lambda i: (0, i))
    left = pl.BlockSpec((2, rank, chunk), lambda i: (0, 0, i))
    outs, shapes = [trace], [f32(rows, points)]
    if edges:
        outs, shapes = outs + [fixed(rows, BLOCK)] * 2, shapes + [f32(rows, BLOCK)] * 2
    return call(
        functools.partial(far_kernel, steps, len(coefs), len(bases) == 2),
        (steps,),
        (flags, *coefs, *weights, *bases),
        [SMEM, *[fixed(2, rows // 8, 8, BLOCK)] * len(coefs), *[left] * len(weights), *[trace] * len(bases)],
        outs,
        shapes,
        len(coefs) * 3 * 4 * rows * points * rank,
    )


def near_call(flags, x, before, after, local, weights, edges):
    rows, points = x.shape
    blocks, depth, width = weights[0].shape
    group = 4 if blocks % 4 == 0 else 1
    steps = blocks // group
    part = pl.BlockSpec((rows, group * BLOCK), lambda i: (0, i))
    near = pl.BlockSpec((group, depth, width), lambda i: (i, 0, 0))
    own = local is not None
    outs, shapes = [part], [f32(rows, points)]
    if edges:
        outs, shapes = outs + [fixed(rows, BLOCK)] * 2, shapes + [f32(rows, BLOCK)] * 2
    return call(
        functools.partial(near_kernel, steps, group, own, edges),
        (steps,),
        (flags, x, before, after, *([local] if own else []), *weights),
        [SMEM, fixed(rows, points), fixed(rows, BLOCK), fixed(rows, BLOCK), *([part] if own else []), near, near],
        outs,
        shapes,
        3 * 2 * rows * blocks * depth * width,
        [pltpu.VMEM((rows, points + 2 * BLOCK), jnp.bfloat16)] * 2,
    )


def split_left(x, factor):
    _, rank, points = x.shape
    part = pl.BlockSpec((1, rank, points), lambda i: (i, 0, 0))
    shapes = [jax.ShapeDtypeStruct(x.shape, jnp.bfloat16)] * 2
    if factor is None:
        return call(split_kernel, (2,), (x,), [part], [part] * 2, shapes)
    args = (x, factor.reshape(1, 1, points))
    return call(scale_kernel, (2,), args, [part, fixed(1, 1, points)], [part] * 2, shapes)


def split_near(x, factor):
    _, blocks, depth, width = x.shape
    group = 3 if blocks % 3 == 0 else 1
    ins = [
        pl.BlockSpec((2, group, depth, width), lambda i: (0, i, 0, 0)),
        pl.BlockSpec((group, 1, width), lambda i: (i, 0, 0)),
    ]
    out = pl.BlockSpec((group, depth, 2 * width), lambda i: (i, 0, 0))
    shapes = [jax.ShapeDtypeStruct((blocks, depth, 2 * width), jnp.bfloat16)] * 2
    return call(pair_kernel, (blocks // group,), (x, factor.reshape(blocks, 1, width)), ins, [out] * 2, shapes)


def on_device(slabs, tiles, local_field, material, contrast, low_left, low_right, near_blocks):
    _, sources, _, points = local_field.shape
    rank = low_left.shape[2]
    rows = 2 * sources
    slab, tile = lax.axis_index("slab"), lax.axis_index("tile")
    flags = jnp.stack([slab == 0, tile == 0, tile == tiles - 1, slab % 2 == 1]).astype(jnp.int32)

    def sent(x, target, across):
        pairs = [
            (s * tiles + t, target(s) * tiles + (t + across) % tiles) for s in range(slabs) for t in range(tiles)
        ]
        return lax.ppermute(x, AXES, pairs)

    def below(x, across=0):
        return sent(x, lambda s: (s + 1) % slabs, across)

    def partner(x, across=0):
        return sent(x, lambda s: s ^ 1, across)

    def beside(x, across):
        return sent(x, lambda s: s, across)

    def total(shares):
        pieces = shares.reshape(tiles, -1, BLOCK)
        parts = lax.all_to_all(pieces, "tile", 0, 0)
        whole = lambda n: fixed(*n.shape)
        copies = call(sum_kernel, (1,), (parts,), [whole(parts)], whole(parts), f32(*parts.shape))
        return lax.all_to_all(copies, "tile", 0, 0).reshape(shares.shape)

    local = local_field[:, :, 0].reshape(rows, points)
    first, last = local[:, :BLOCK], local[:, points - BLOCK :]
    factor = jnp.sum(
        jnp.where(material[0][None, :] == jnp.arange(contrast.shape[0], dtype=jnp.int32)[:, None], contrast[:, None], 0.0),
        axis=0,
    )
    right = split_left(low_right[0], None)
    left = split_left(low_left[0], factor)
    near = split_near(near_blocks[0], factor)

    w, w_first, w_last = local, first, last
    arrived = jnp.zeros_like(local)
    w_arrived = partner(w)
    shares = right_call(flags, (arrived, w_arrived), right)
    c = total(shares)
    v = near_call(flags, w_arrived, partner(w_last, 1), partner(w_first, -1), local, near, False)[0]
    t, first, last = far_call(flags, (c,), left, (w, v), True)

    upper_flat = (partner(low_left[0]) * partner(factor)).reshape(2 * rank, points)
    m = total(right_call(flags, (upper_flat,), right))
    u_before = beside(upper_flat[:, points - BLOCK :], 1)
    u_after = beside(upper_flat[:, :BLOCK], -1)
    q = near_call(flags, upper_flat, u_before, u_after, None, near, False)[0]
    g = far_call(flags, (m,), left, (q,), False)[0]
    through = split_left(g.reshape(2, rank, points), None)

    for _ in range(1, slabs // 2):
        arrived = below(t)
        w, w_first, w_last = near_call(flags, arrived, below(last, 1), below(first, -1), local, near, True)
        w_arrived = partner(w)
        c = total(right_call(flags, (arrived, w_arrived), right))
        v = near_call(flags, w_arrived, partner(w_last, 1), partner(w_first, -1), local, near, False)[0]
        t, first, last = far_call(flags, (c, partner(c)), (*left, *through), (w, v), True)
    return t.reshape(2, sources, 1, points)


def solution(mesh):
    slabs, tiles = mesh.shape["slab"], mesh.shape["tile"]
    return jax.shard_map(
        functools.partial(on_device, slabs, tiles),
        mesh=mesh,
        in_specs=(
            P(None, None, "slab", "tile"),
            P("slab", "tile"),
            P(),
            P("slab", None, None, "tile"),
            P("slab", None, "tile", None),
            P("slab", None, "tile", None, None),
        ),
        out_specs=P(None, None, "slab", "tile"),
        check_vma=False,
    )
```

time: 1410 us -> 338 us (0.24)
  waiting for transfers between devices: 1040 us -> 55.2 us
  matrix products: 178 us -> 0 us
  Pallas kernels: 0 us -> 61.7 us
  blocking collectives: 0 us -> 53.3 us
  starting transfers between devices: 99.3 us -> 114 us
    psum x8 -> x0, waiting for transfers between devices: 972 us -> none  [total_coefficients(): return lax.psum(partial_sums, 'tile')]
    dot_general x97 -> x0, matrix products: 178 us -> none  [the longest x24 55.7 us: complex_product(): jnp.einsum(pattern, first[1], second[1], precision=high)]
    pallas_call x0 -> x27, Pallas kernels: none -> 61.7 us  [call(): pl.pallas_call(body, grid=grid, in_specs=ins, out_specs=outs, out_shape=o...]
    all_to_all x0 -> x3, blocking collectives: none -> 53.3 us  [total(): parts = lax.all_to_all(pieces, 'tile', 0, 0)]
    ppermute x24 -> x28, waiting for transfers between devices: 71.2 us -> 29.4 us  [sent(): return lax.ppermute(x, AXES, pairs)]
    all_to_all x0 -> x7, starting transfers between devices: none -> 41.6 us  [the longest x5 25.6 us: total(): return lax.all_to_all(copies, 'tile', 0, 0).reshape(shares.shape)]
    unnamed x3 -> x129, local copies, waits for them, and re-layouts: 2.08 us -> 41.7 us
    ppermute x24 -> x28, starting transfers between devices: 98.9 us -> 72.1 us  [sent(): return lax.ppermute(x, AXES, pairs)]
  transfers between devices with their start and end apart: 32 -> 35, of which waited for: 16 -> 16; matrix products, arithmetic and copies ran while one was open for 13% -> 1% of each run, Pallas kernels for 0% -> 13%
where the time goes in v1:
time: 338 us; the launch traced here: 333 us
  starting transfers between devices  114 us (34%)
  Pallas kernels  61.7 us (18%)
  waiting for transfers between devices  55.2 us (16%)
  blocking collectives  53.3 us (16%)
  local copies, waits for them, and re-layouts  45.2 us (13%)
    ppermute x28, starting transfers between devices, sent(): return lax.ppermute(x, AXES, pairs)  72.1 us
    pallas_call x27, Pallas kernels, call(): pl.pallas_call(body, grid=grid, in_specs=ins, out_specs=outs, out_shape=o...  61.7 us
    all_to_all x3, blocking collectives, total(): parts = lax.all_to_all(pieces, 'tile', 0, 0)  53.3 us
    unnamed x129, local copies, waits for them, and re-layouts  41.7 us
    ppermute x28, waiting for transfers between devices, sent(): return lax.ppermute(x, AXES, pairs)  29.4 us
    all_to_all x5, starting transfers between devices, total(): return lax.all_to_all(copies, 'tile', 0, 0).reshape(shares.shape)  25.6 us
    all_to_all x2, starting transfers between devices, total(): parts = lax.all_to_all(pieces, 'tile', 0, 0)  16 us
    all_to_all x2, waiting for transfers between devices, total(): parts = lax.all_to_all(pieces, 'tile', 0, 0)  13.4 us
  transfers between devices with their start and end apart: 35, of which 16 were waited for; matrix products, arithmetic and copies ran while one was open for 1% of the time, Pallas kernels for 13%

profile of v1, /device:TPU:1, one launch (start us, length us, event | category | flops | bytes accessed | tf_op | source)
XLA Modules:
  0.0 332.8 jit_solution(18235773313989228300)
XLA Ops:
  1.2 3.3 collective-permute-start
  12.5 18.2 %all_to_all.50.parts_ref = f32[32,8,128]{2,1,0:T(8,128)S(1)} all-to-all(f32[32,8,128]{2,1,0:T(8,128)S(1)} %bitcast.48), channel_id=1, replica_groups=mesh['slab'=8,'tile'=32] {'tile'}, dimensions={0} | all-to-all | bytes 262144 | tf_op jit(solution)/shard_map/all_to_all | solution.py:305
  31.4 4.4 %all-to-all-start.1 = ((f32[32,8,128]{2,1,0:T(8,128)}), f32[32,8,128]{2,1,0:T(8,128)S(1)}, u32[]{:S(2)}, u32[]{:S(2)}) async-start(f32[32,8,128]{2,1,0:T(8,128)} %shard_map.66), calls=%async_computation.1 | async-start | bytes 262144 | tf_op jit(solution)/shard_map/all_to_all | solution.py:308
  36.4 6.4 %collective-permute-start.2 = (f32[128,128]{1,0:T(8,128)}, f32[128,128]{1,0:T(8,128)S(1)}, u32[]{:S(2)}, u32[]{:S(2)}) collective-permute-start(f32[128,128]{1,0:T(8,128)} %get-tuple-element.61), channel_id=1, source_target_pairs={{0,63},{1,32},{2,33},{3,34},{4,35},{5,36},{6,37},{7,38},{8,39},{9,... | collective-permute-start | bytes 196616 | tf_op jit(solution)/shard_map/ppermute | solution.py:292
  51.7 2.6 shard_map.69.refs_4_
  62.9 6.2 %collective-permute-start.5 = (f32[128,128]{1,0:T(8,128)S(1)}, f32[128,128]{1,0:T(8,128)S(1)}, u32[]{:S(2)}, u32[]{:S(2)}) collective-permute-start(f32[128,128]{1,0:T(8,128)S(1)} %get-tuple-element.40), channel_id=1, source_target_pairs={{0,63},{1,32},{2,33},{3,34},{4,35},{5,36},{6,37},{7,38},{8,39},{9,... | collective-permute-start | bytes 196616 | tf_op jit(solution)/shard_map/ppermute | solution.py:292
  70.4 2.7 collective-permute-done.3.x_ref.refs_0_
  73.1 2.6 shard_map.71
  75.8 4.0 %collective-permute-start.6 = (f32[128,1536]{1,0:T(8,128)S(1)}, f32[128,1536]{1,0:T(8,128)S(1)}, u32[]{:S(2)}, u32[]{:S(2)}) collective-permute-start(f32[128,1536]{1,0:T(8,128)S(1)} %get-tuple-element.41.refs_6_), channel_id=1, source_target_pairs={{0,32},{1,33},{2,34},{3,35},{4,36},{5,37},{6,38},{7,39},{8,40},{9,... | collective-permute-start | bytes 2359304 | tf_op jit(solution)/shard_map/ppermute | solution.py:292
  81.6 2.6 shard_map.72
  84.3 6.7 %all-to-all-start.2 = ((f32[32,8,128]{2,1,0:T(8,128)}), f32[32,8,128]{2,1,0:T(8,128)S(1)}, u32[]{:S(2)}, u32[]{:S(2)}) async-start(f32[32,8,128]{2,1,0:T(8,128)} %bitcast.9), calls=%async_computation.2 | async-start | bytes 262144 | tf_op jit(solution)/shard_map/all_to_all | solution.py:305
  93.8 4.0 %shard_map.74 = f32[2,64,8,128]{3,2,1,0:T(8,128)S(1)} custom-call(s32[4]{0:T(128)S(1)} %add_convert_fusion.flags, f32[512,1536]{1,0:T(8,128)S(1)} %bitcast.33, bf16[2,1536,256]{2,1,0:T(8,128)(2,1)S(1)} %copy-done.21, bf16[2,1536,256]{2,1,0:T(8,128)(2,1)S(1)} %copy-done.26), custom_call_target="tpu_custom_call" | custom-call | flops 2415919104 | bytes 6291472 | tf_op jit(solution)/shard_map/pallas_call | solution.py:175
  100.3 9.4 %all-to-all-start.4 = ((f32[32,32,128]{2,1,0:T(8,128)}), f32[32,32,128]{2,1,0:T(8,128)}, u32[]{:S(2)}, u32[]{:S(2)}) async-start(f32[32,32,128]{2,1,0:T(8,128)} %bitcast.50), calls=%async_computation.4 | async-start | bytes 1048576 | tf_op jit(solution)/shard_map/all_to_all | solution.py:305
  110.3 13.4 %all-to-all-done.4.parts_ref = f32[32,32,128]{2,1,0:T(8,128)} async-done(((f32[32,32,128]{2,1,0:T(8,128)}), f32[32,32,128]{2,1,0:T(8,128)}, u32[]{:S(2)}, u32[]{:S(2)}) %all-to-all-start.4) | async-done | bytes 524320 | tf_op jit(solution)/shard_map/all_to_all | solution.py:305
  123.7 7.9 %all-to-all-start.3 = ((f32[32,8,128]{2,1,0:T(8,128)}), f32[32,8,128]{2,1,0:T(8,128)S(1)}, u32[]{:S(2)}, u32[]{:S(2)}) async-start(f32[32,8,128]{2,1,0:T(8,128)} %shard_map.73), calls=%async_computation.3 | async-start | bytes 262144 | tf_op jit(solution)/shard_map/all_to_all | solution.py:308
  133.6 7.2 %all-to-all-done.3 = f32[32,8,128]{2,1,0:T(8,128)S(1)} async-done(((f32[32,8,128]{2,1,0:T(8,128)}), f32[32,8,128]{2,1,0:T(8,128)S(1)}, u32[]{:S(2)}, u32[]{:S(2)}) %all-to-all-start.3) | async-done | bytes 131104 | tf_op jit(solution)/shard_map/all_to_all | solution.py:308
  140.8 4.6 %all-to-all-start.5 = ((f32[32,32,128]{2,1,0:T(8,128)}), f32[32,32,128]{2,1,0:T(8,128)}, u32[]{:S(2)}, u32[]{:S(2)}) async-start(f32[32,32,128]{2,1,0:T(8,128)} %copy-done.54), calls=%async_computation.5 | async-start | bytes 1048576 | tf_op jit(solution)/shard_map/all_to_all | solution.py:308
  146.5 4.6 %collective-permute-start.11 = (f32[512,128]{1,0:T(8,128)S(1)}, f32[512,128]{1,0:T(8,128)S(1)}, u32[]{:S(2)}, u32[]{:S(2)}) collective-permute-start(f32[512,128]{1,0:T(8,128)S(1)} %get-tuple-element.59), channel_id=1, source_target_pairs={{0,31},{1,0},{2,1},{3,2},{4,3},{5,4},{6,5},{7,6},{8,7},{9,8},{10,9... | collective-permute-start | bytes 786440 | tf_op jit(solution)/shard_map/ppermute | solution.py:292
  152.4 6.8 %collective-permute-start.13 = (f32[128,128]{1,0:T(8,128)S(1)}, f32[128,128]{1,0:T(8,128)S(1)}, u32[]{:S(2)}, u32[]{:S(2)}) collective-permute-start(f32[128,128]{1,0:T(8,128)S(1)} %get-tuple-element.45), channel_id=1, source_target_pairs={{0,63},{1,32},{2,33},{3,34},{4,35},{5,36},{6,37},{7,38},{8,39},{9,... | collective-permute-start | bytes 196616 | tf_op jit(solution)/shard_map/ppermute | solution.py:292
  159.3 10.0 %collective-permute-done.12.before_ref = f32[128,128]{1,0:T(8,128)S(1)} collective-permute-done((f32[128,128]{1,0:T(8,128)S(1)}, f32[128,128]{1,0:T(8,128)S(1)}, u32[]{:S(2)}, u32[]{:S(2)}) %collective-permute-start.12) | collective-permute-done | bytes 65568 | tf_op jit(solution)/shard_map/ppermute | solution.py:292
  172.0 2.6 shard_map.79.refs_7_
  175.5 8.1 %shard_map.76.refs_3_ = f32[512,1536]{1,0:T(8,128)S(1)} custom-call(s32[4]{0:T(128)S(1)} %add_convert_fusion.flags, f32[512,1536]{1,0:T(8,128)} %bitcast.35, f32[512,128]{1,0:T(8,128)S(1)} %collective-permute-done.10.before_ref, f32[512,128]{1,0:T(8,128)S(1)} %collective-permute-done.11.after_ref, ...), custom_call_target="tpu_custom_call" | custom-call | flops 3623878656 | bytes 8388624 | tf_op jit(solution)/shard_map/pallas_call | solution.py:175
  190.0 4.6 %shard_map.77 = f32[512,1536]{1,0:T(8,128)S(1)} custom-call(s32[4]{0:T(128)S(1)} %add_convert_fusion.flags, f32[2,64,8,128]{3,2,1,0:T(8,128)} %bitcast.13.refs_0_, bf16[2,256,1536]{2,1,0:T(8,128)(2,1)S(1)} %copy-done.9, bf16[2,256,1536]{2,1,0:T(8,128)(2,1)S(1)} %copy-done.15, f32[512,1536]{1,0:T(8,128)S(1)} %copy-done.38), custom_call_target="tpu_custom_call" | custom-call | flops 2415919104 | bytes 6815760 | tf_op jit(solution)/shard_map/pallas_call | solution.py:175
  197.6 2.8 shard_map.80
  200.9 6.1 %collective-permute-start.16 = (f32[128,128]{1,0:T(8,128)S(1)}, f32[128,128]{1,0:T(8,128)S(1)}, u32[]{:S(2)}, u32[]{:S(2)}) collective-permute-start(f32[128,128]{1,0:T(8,128)S(1)} %get-tuple-element.48), channel_id=1, source_target_pairs={{0,63},{1,32},{2,33},{3,34},{4,35},{5,36},{6,37},{7,38},{8,39},{9,... | collective-permute-start | bytes 196616 | tf_op jit(solution)/shard_map/ppermute | solution.py:292
  208.4 2.9 collective-permute-done.14.x_ref.refs_0_
  211.3 2.6 shard_map.81
  213.9 3.8 %collective-permute-start.17 = (f32[128,1536]{1,0:T(8,128)S(1)}, f32[128,1536]{1,0:T(8,128)S(1)}, u32[]{:S(2)}, u32[]{:S(2)}) collective-permute-start(f32[128,1536]{1,0:T(8,128)S(1)} %get-tuple-element.49.refs_6_), channel_id=1, source_target_pairs={{0,32},{1,33},{2,34},{3,35},{4,36},{5,37},{6,38},{7,39},{8,40},{9,... | collective-permute-start | bytes 2359304 | tf_op jit(solution)/shard_map/ppermute | solution.py:292
  221.7 22.8 %all_to_all.51.parts_ref = f32[32,8,128]{2,1,0:T(8,128)S(1)} all-to-all(f32[32,8,128]{2,1,0:T(8,128)S(1)} %bitcast.49), channel_id=1, replica_groups=mesh['slab'=8,'tile'=32] {'tile'}, dimensions={0} | all-to-all | bytes 262144 | tf_op jit(solution)/shard_map/all_to_all | solution.py:305
  245.1 4.4 %all-to-all-start.7 = ((f32[32,8,128]{2,1,0:T(8,128)}), f32[32,8,128]{2,1,0:T(8,128)S(1)}, u32[]{:S(2)}, u32[]{:S(2)}) async-start(f32[32,8,128]{2,1,0:T(8,128)} %shard_map.83), calls=%async_computation.7 | async-start | bytes 262144 | tf_op jit(solution)/shard_map/all_to_all | solution.py:308
  249.5 3.0 collective-permute-start.19
  252.4 3.6 %collective-permute-start.20 = (f32[128,128]{1,0:T(8,128)S(1)}, f32[128,128]{1,0:T(8,128)S(1)}, u32[]{:S(2)}, u32[]{:S(2)}) collective-permute-start(f32[128,128]{1,0:T(8,128)S(1)} %get-tuple-element.51), channel_id=1, source_target_pairs={{0,63},{1,32},{2,33},{3,34},{4,35},{5,36},{6,37},{7,38},{8,39},{9,... | collective-permute-start | bytes 196616 | tf_op jit(solution)/shard_map/ppermute | solution.py:292
  256.0 2.6 all-to-all-done.7
  258.7 3.5 %collective-permute-start.18 = (f32[2,16,8,128]{3,2,1,0:T(8,128)S(1)}, f32[2,16,8,128]{3,2,1,0:T(8,128)S(1)}, u32[]{:S(2)}, u32[]{:S(2)}) collective-permute-start(f32[2,16,8,128]{3,2,1,0:T(8,128)S(1)} %bitcast.44), channel_id=1, source_target_pairs={{0,32},{1,33},{2,34},{3,35},{4,36},{5,37},{6,38},{7,39},{8,40},{9,... | collective-permute-start | bytes 393224 | tf_op jit(solution)/shard_map/ppermute | solution.py:292
  265.0 2.6 shard_map.84.refs_7_
  268.0 2.8 shard_map.85
  270.9 4.7 %collective-permute-start.23 = (f32[128,128]{1,0:T(8,128)S(1)}, f32[128,128]{1,0:T(8,128)S(1)}, u32[]{:S(2)}, u32[]{:S(2)}) collective-permute-start(f32[128,128]{1,0:T(8,128)S(1)} %get-tuple-element.54), channel_id=1, source_target_pairs={{0,63},{1,32},{2,33},{3,34},{4,35},{5,36},{6,37},{7,38},{8,39},{9,... | collective-permute-start | bytes 196616 | tf_op jit(solution)/shard_map/ppermute | solution.py:292
  277.9 3.2 collective-permute-done.21.x_ref.refs_0_
  281.2 2.6 shard_map.86
  283.8 3.8 %collective-permute-start.24 = (f32[128,1536]{1,0:T(8,128)S(1)}, f32[128,1536]{1,0:T(8,128)S(1)}, u32[]{:S(2)}, u32[]{:S(2)}) collective-permute-start(f32[128,1536]{1,0:T(8,128)S(1)} %get-tuple-element.55.refs_6_), channel_id=1, source_target_pairs={{0,32},{1,33},{2,34},{3,35},{4,36},{5,37},{6,38},{7,39},{8,40},{9,... | collective-permute-start | bytes 2359304 | tf_op jit(solution)/shard_map/ppermute | solution.py:292
  291.5 12.3 %all_to_all.52.parts_ref = f32[32,8,128]{2,1,0:T(8,128)S(1)} all-to-all(f32[32,8,128]{2,1,0:T(8,128)S(1)} %bitcast.47), channel_id=1, replica_groups=mesh['slab'=8,'tile'=32] {'tile'}, dimensions={0} | all-to-all | bytes 262144 | tf_op jit(solution)/shard_map/all_to_all | solution.py:305
  304.6 4.4 %all-to-all-start.9 = ((f32[32,8,128]{2,1,0:T(8,128)}), f32[32,8,128]{2,1,0:T(8,128)S(1)}, u32[]{:S(2)}, u32[]{:S(2)}) async-start(f32[32,8,128]{2,1,0:T(8,128)} %shard_map.88), calls=%async_computation.9 | async-start | bytes 262144 | tf_op jit(solution)/shard_map/all_to_all | solution.py:308
  308.9 3.0 collective-permute-start.26
  311.9 3.6 %collective-permute-start.27 = (f32[128,128]{1,0:T(8,128)S(1)}, f32[128,128]{1,0:T(8,128)S(1)}, u32[]{:S(2)}, u32[]{:S(2)}) collective-permute-start(f32[128,128]{1,0:T(8,128)S(1)} %get-tuple-element.57), channel_id=1, source_target_pairs={{0,63},{1,32},{2,33},{3,34},{4,35},{5,36},{6,37},{7,38},{8,39},{9,... | collective-permute-start | bytes 196616 | tf_op jit(solution)/shard_map/ppermute | solution.py:292
  315.5 2.6 all-to-all-done.9
  318.1 3.5 %collective-permute-start.25 = (f32[2,16,8,128]{3,2,1,0:T(8,128)S(1)}, f32[2,16,8,128]{3,2,1,0:T(8,128)S(1)}, u32[]{:S(2)}, u32[]{:S(2)}) collective-permute-start(f32[2,16,8,128]{3,2,1,0:T(8,128)S(1)} %bitcast.42), channel_id=1, source_target_pairs={{0,32},{1,33},{2,34},{3,35},{4,36},{5,37},{6,38},{7,39},{8,40},{9,... | collective-permute-start | bytes 393224 | tf_op jit(solution)/shard_map/ppermute | solution.py:292
  324.5 2.6 shard_map.89.refs_7_
  327.4 3.4 %shard_map.90 = (f32[128,1536]{1,0:T(8,128)S(1)}, f32[128,128]{1,0:T(8,128)}, f32[128,128]{1,0:T(8,128)}) custom-call(s32[4]{0:T(128)S(1)} %add_convert_fusion.flags, f32[2,16,8,128]{3,2,1,0:T(8,128)S(1)} %bitcast.43, f32[2,16,8,128]{3,2,1,0:T(8,128)S(1)} %collective-permute-done.25.refs_1_, bf16[2,256,1536]{2,1,0:T(8,128)(2,1)S(1)} %copy-done.12, ...), custom_call_target="tpu_custom_call" | custom-call | flops 1207959552 | bytes 8126480 | tf_op jit(solution)/shard_map/pallas_call | solution.py:175
  (191 shorter events, 75.5 us)
Async XLA Ops:
  1.2 5.9 %collective-permute-start = (f32[128,1536]{1,0:T(8,128)S(1)}, f32[128,1536]{1,0:T(8,128)S(1)}, u32[]{:S(2)}, u32[]{:S(2)}) collective-permute-start(f32[128,1536]{1,0:T(8,128)S(1)} %bitcast.21), channel_id=1, source_target_pairs={{0,32},{1,33},{2,34},{3,35},{4,36},{5,37},{6,38},{7,39},{8,40},{9,... | collective-permute-start | bytes 2359304 | tf_op jit(solution)/shard_map/ppermute | solution.py:292
  4.5 86.5 %collective-permute-start.8 = (f32[2,256,1536]{2,1,0:T(8,128)}, f32[2,256,1536]{2,1,0:T(8,128)}, u32[]{:S(2)}, u32[]{:S(2)}) collective-permute-start(f32[2,256,1536]{2,1,0:T(8,128)} %bitcast.37), channel_id=1, source_target_pairs={{0,32},{1,33},{2,34},{3,35},{4,36},{5,37},{6,38},{7,39},{8,40},{9,... | collective-permute-start | bytes 9437192 | tf_op jit(solution)/shard_map/ppermute | solution.py:292
  9.3 33.5 %copy-start.62 = (s32[1,1536]{1,0:T(1,128)S(1)}, s32[1,1536]{1,0:T(1,128)}, u32[]{:S(2)}) copy-start(s32[1,1536]{1,0:T(1,128)} %param.7) | copy-start | bytes 18436
  9.3 33.6 %copy-start.63 = (f32[16]{0:T(128)S(1)}, f32[16]{0:T(128)}, u32[]{:S(2)}) copy-start(f32[16]{0:T(128)} %param.8) | copy-start | bytes 196
  31.4 25.2 %all-to-all-start.1 = ((f32[32,8,128]{2,1,0:T(8,128)}), f32[32,8,128]{2,1,0:T(8,128)S(1)}, u32[]{:S(2)}, u32[]{:S(2)}) async-start(f32[32,8,128]{2,1,0:T(8,128)} %shard_map.66), calls=%async_computation.1 | async-start | bytes 262144 | tf_op jit(solution)/shard_map/all_to_all | solution.py:308
  36.4 15.2 %collective-permute-start.2 = (f32[128,128]{1,0:T(8,128)}, f32[128,128]{1,0:T(8,128)S(1)}, u32[]{:S(2)}, u32[]{:S(2)}) collective-permute-start(f32[128,128]{1,0:T(8,128)} %get-tuple-element.61), channel_id=1, source_target_pairs={{0,63},{1,32},{2,33},{3,34},{4,35},{5,36},{6,37},{7,38},{8,39},{9,... | collective-permute-start | bytes 196616 | tf_op jit(solution)/shard_map/ppermute | solution.py:292
  42.8 8.9 %collective-permute-start.1 = (f32[128,128]{1,0:T(8,128)S(1)}, f32[128,128]{1,0:T(8,128)S(1)}, u32[]{:S(2)}, u32[]{:S(2)}) collective-permute-start(f32[128,128]{1,0:T(8,128)S(1)} %get-tuple-element.62), channel_id=1, source_target_pairs={{0,33},{1,34},{2,35},{3,36},{4,37},{5,38},{6,39},{7,40},{8,41},{9,... | collective-permute-start | bytes 196616 | tf_op jit(solution)/shard_map/ppermute | solution.py:292
  56.6 16.5 %copy-start.1 = (bf16[12,384,256]{2,1,0:T(8,128)(2,1)S(1)}, bf16[12,384,256]{2,1,0:T(8,128)(2,1)}, u32[]{:S(2)}) copy-start(bf16[12,384,256]{2,1,0:T(8,128)(2,1)} %copy-done) | copy-start | bytes 7077892
  62.8 10.4 %collective-permute-start.3 = (f32[128,1536]{1,0:T(8,128)S(1)}, f32[128,1536]{1,0:T(8,128)S(1)}, u32[]{:S(2)}, u32[]{:S(2)}) collective-permute-start(f32[128,1536]{1,0:T(8,128)S(1)} %get-tuple-element.38), channel_id=1, source_target_pairs={{0,32},{1,33},{2,34},{3,35},{4,36},{5,37},{6,38},{7,39},{8,40},{9,... | collective-permute-start | bytes 2359304 | tf_op jit(solution)/shard_map/ppermute | solution.py:292
  62.8 7.1 %collective-permute-start.4 = (f32[128,128]{1,0:T(8,128)S(1)}, f32[128,128]{1,0:T(8,128)S(1)}, u32[]{:S(2)}, u32[]{:S(2)}) collective-permute-start(f32[128,128]{1,0:T(8,128)S(1)} %get-tuple-element.39), channel_id=1, source_target_pairs={{0,33},{1,34},{2,35},{3,36},{4,37},{5,38},{6,39},{7,40},{8,41},{9,... | collective-permute-start | bytes 196616 | tf_op jit(solution)/shard_map/ppermute | solution.py:292
  62.9 18.7 %copy-start.20 = (bf16[2,1536,256]{2,1,0:T(8,128)(2,1)S(1)}, bf16[2,1536,256]{2,1,0:T(8,128)(2,1)}, u32[]{:S(2)}) copy-start(bf16[2,1536,256]{2,1,0:T(8,128)(2,1)} %copy-done.19) | copy-start | bytes 4718596
  62.9 18.7 %copy-start.25 = (bf16[2,1536,256]{2,1,0:T(8,128)(2,1)S(1)}, bf16[2,1536,256]{2,1,0:T(8,128)(2,1)}, u32[]{:S(2)}) copy-start(bf16[2,1536,256]{2,1,0:T(8,128)(2,1)} %copy-done.24) | copy-start | bytes 4718596
  62.9 7.5 %collective-permute-start.5 = (f32[128,128]{1,0:T(8,128)S(1)}, f32[128,128]{1,0:T(8,128)S(1)}, u32[]{:S(2)}, u32[]{:S(2)}) collective-permute-start(f32[128,128]{1,0:T(8,128)S(1)} %get-tuple-element.40), channel_id=1, source_target_pairs={{0,63},{1,32},{2,33},{3,34},{4,35},{5,36},{6,37},{7,38},{8,39},{9,... | collective-permute-start | bytes 196616 | tf_op jit(solution)/shard_map/ppermute | solution.py:292
  75.7 8.5 %copy-start.55 = (f32[128,1536]{1,0:T(8,128)}, f32[128,1536]{1,0:T(8,128)S(1)}, u32[]{:S(2)}) copy-start(f32[128,1536]{1,0:T(8,128)S(1)} %get-tuple-element.41.refs_6_) | copy-start | bytes 2359300
  75.8 5.9 %collective-permute-start.6 = (f32[128,1536]{1,0:T(8,128)S(1)}, f32[128,1536]{1,0:T(8,128)S(1)}, u32[]{:S(2)}, u32[]{:S(2)}) collective-permute-start(f32[128,1536]{1,0:T(8,128)S(1)} %get-tuple-element.41.refs_6_), channel_id=1, source_target_pairs={{0,32},{1,33},{2,34},{3,35},{4,36},{5,37},{6,38},{7,39},{8,40},{9,... | collective-permute-start | bytes 2359304 | tf_op jit(solution)/shard_map/ppermute | solution.py:292
  79.7 11.3 %collective-permute-start.9 = (f32[1536]{0:T(1024)S(1)}, f32[1536]{0:T(1024)S(1)}, u32[]{:S(2)}, u32[]{:S(2)}) collective-permute-start(f32[1536]{0:T(1024)S(1)} %select_reduce_fusion), channel_id=1, source_target_pairs={{0,32},{1,33},{2,34},{3,35},{4,36},{5,37},{6,38},{7,39},{8,40},{9,... | collective-permute-start | bytes 18440 | tf_op jit(solution)/shard_map/ppermute | solution.py:292
  84.3 16.0 %all-to-all-start.2 = ((f32[32,8,128]{2,1,0:T(8,128)}), f32[32,8,128]{2,1,0:T(8,128)S(1)}, u32[]{:S(2)}, u32[]{:S(2)}) async-start(f32[32,8,128]{2,1,0:T(8,128)} %bitcast.9), calls=%async_computation.2 | async-start | bytes 262144 | tf_op jit(solution)/shard_map/all_to_all | solution.py:305
  100.3 23.4 %all-to-all-start.4 = ((f32[32,32,128]{2,1,0:T(8,128)}), f32[32,32,128]{2,1,0:T(8,128)}, u32[]{:S(2)}, u32[]{:S(2)}) async-start(f32[32,32,128]{2,1,0:T(8,128)} %bitcast.50), calls=%async_computation.4 | async-start | bytes 1048576 | tf_op jit(solution)/shard_map/all_to_all | solution.py:305
  123.7 17.1 %all-to-all-start.3 = ((f32[32,8,128]{2,1,0:T(8,128)}), f32[32,8,128]{2,1,0:T(8,128)S(1)}, u32[]{:S(2)}, u32[]{:S(2)}) async-start(f32[32,8,128]{2,1,0:T(8,128)} %shard_map.73), calls=%async_computation.3 | async-start | bytes 262144 | tf_op jit(solution)/shard_map/all_to_all | solution.py:308
  140.8 44.6 %all-to-all-start.5 = ((f32[32,32,128]{2,1,0:T(8,128)}), f32[32,32,128]{2,1,0:T(8,128)}, u32[]{:S(2)}, u32[]{:S(2)}) async-start(f32[32,32,128]{2,1,0:T(8,128)} %copy-done.54), calls=%async_computation.5 | async-start | bytes 1048576 | tf_op jit(solution)/shard_map/all_to_all | solution.py:308
  146.5 29.1 %collective-permute-start.11 = (f32[512,128]{1,0:T(8,128)S(1)}, f32[512,128]{1,0:T(8,128)S(1)}, u32[]{:S(2)}, u32[]{:S(2)}) collective-permute-start(f32[512,128]{1,0:T(8,128)S(1)} %get-tuple-element.59), channel_id=1, source_target_pairs={{0,31},{1,0},{2,1},{3,2},{4,3},{5,4},{6,5},{7,6},{8,7},{9,8},{10,9... | collective-permute-start | bytes 786440 | tf_op jit(solution)/shard_map/ppermute | solution.py:292
  151.1 24.4 %collective-permute-start.10 = (f32[512,128]{1,0:T(8,128)S(1)}, f32[512,128]{1,0:T(8,128)S(1)}, u32[]{:S(2)}, u32[]{:S(2)}) collective-permute-start(f32[512,128]{1,0:T(8,128)S(1)} %get-tuple-element.60), channel_id=1, source_target_pairs={{0,1},{1,2},{2,3},{3,4},{4,5},{5,6},{6,7},{7,8},{8,9},{9,10},{10,1... | collective-permute-start | bytes 786440 | tf_op jit(solution)/shard_map/ppermute | solution.py:292
  151.1 18.1 %collective-permute-start.12 = (f32[128,128]{1,0:T(8,128)S(1)}, f32[128,128]{1,0:T(8,128)S(1)}, u32[]{:S(2)}, u32[]{:S(2)}) collective-permute-start(f32[128,128]{1,0:T(8,128)S(1)} %get-tuple-element.44), channel_id=1, source_target_pairs={{0,33},{1,34},{2,35},{3,36},{4,37},{5,38},{6,39},{7,40},{8,41},{9,... | collective-permute-start | bytes 196616 | tf_op jit(solution)/shard_map/ppermute | solution.py:292
  152.4 16.8 %collective-permute-start.13 = (f32[128,128]{1,0:T(8,128)S(1)}, f32[128,128]{1,0:T(8,128)S(1)}, u32[]{:S(2)}, u32[]{:S(2)}) collective-permute-start(f32[128,128]{1,0:T(8,128)S(1)} %get-tuple-element.45), channel_id=1, source_target_pairs={{0,63},{1,32},{2,33},{3,34},{4,35},{5,36},{6,37},{7,38},{8,39},{9,... | collective-permute-start | bytes 196616 | tf_op jit(solution)/shard_map/ppermute | solution.py:292
  175.5 19.7 %collective-permute-start.7 = (f32[2,16,8,128]{3,2,1,0:T(8,128)S(1)}, f32[2,16,8,128]{3,2,1,0:T(8,128)S(1)}, u32[]{:S(2)}, u32[]{:S(2)}) collective-permute-start(f32[2,16,8,128]{3,2,1,0:T(8,128)S(1)} %bitcast.40), channel_id=1, source_target_pairs={{0,32},{1,33},{2,34},{3,35},{4,36},{5,37},{6,38},{7,39},{8,40},{9,... | collective-permute-start | bytes 393224 | tf_op jit(solution)/shard_map/ppermute | solution.py:292
  197.6 13.7 %copy-start.3 = (bf16[12,384,256]{2,1,0:T(8,128)(2,1)S(1)}, bf16[12,384,256]{2,1,0:T(8,128)(2,1)}, u32[]{:S(2)}) copy-start(bf16[12,384,256]{2,1,0:T(8,128)(2,1)} %copy-done) | copy-start | bytes 7077892
  200.5 10.8 %collective-permute-start.14 = (f32[128,1536]{1,0:T(8,128)S(1)}, f32[128,1536]{1,0:T(8,128)S(1)}, u32[]{:S(2)}, u32[]{:S(2)}) collective-permute-start(f32[128,1536]{1,0:T(8,128)S(1)} %get-tuple-element.46), channel_id=1, source_target_pairs={{0,32},{1,33},{2,34},{3,35},{4,36},{5,37},{6,38},{7,39},{8,40},{9,... | collective-permute-start | bytes 2359304 | tf_op jit(solution)/shard_map/ppermute | solution.py:292
  200.9 7.0 %collective-permute-start.15 = (f32[128,128]{1,0:T(8,128)S(1)}, f32[128,128]{1,0:T(8,128)S(1)}, u32[]{:S(2)}, u32[]{:S(2)}) collective-permute-start(f32[128,128]{1,0:T(8,128)S(1)} %get-tuple-element.47), channel_id=1, source_target_pairs={{0,33},{1,34},{2,35},{3,36},{4,37},{5,38},{6,39},{7,40},{8,41},{9,... | collective-permute-start | bytes 196616 | tf_op jit(solution)/shard_map/ppermute | solution.py:292
  200.9 18.7 %copy-start.22 = (bf16[2,1536,256]{2,1,0:T(8,128)(2,1)S(1)}, bf16[2,1536,256]{2,1,0:T(8,128)(2,1)}, u32[]{:S(2)}) copy-start(bf16[2,1536,256]{2,1,0:T(8,128)(2,1)} %copy-done.19) | copy-start | bytes 4718596
  200.9 18.7 %copy-start.27 = (bf16[2,1536,256]{2,1,0:T(8,128)(2,1)S(1)}, bf16[2,1536,256]{2,1,0:T(8,128)(2,1)}, u32[]{:S(2)}) copy-start(bf16[2,1536,256]{2,1,0:T(8,128)(2,1)} %copy-done.24) | copy-start | bytes 4718596
  200.9 7.4 %collective-permute-start.16 = (f32[128,128]{1,0:T(8,128)S(1)}, f32[128,128]{1,0:T(8,128)S(1)}, u32[]{:S(2)}, u32[]{:S(2)}) collective-permute-start(f32[128,128]{1,0:T(8,128)S(1)} %get-tuple-element.48), channel_id=1, source_target_pairs={{0,63},{1,32},{2,33},{3,34},{4,35},{5,36},{6,37},{7,38},{8,39},{9,... | collective-permute-start | bytes 196616 | tf_op jit(solution)/shard_map/ppermute | solution.py:292
  213.9 7.8 %copy-start.59 = (f32[128,1536]{1,0:T(8,128)}, f32[128,1536]{1,0:T(8,128)S(1)}, u32[]{:S(2)}) copy-start(f32[128,1536]{1,0:T(8,128)S(1)} %get-tuple-element.49.refs_6_) | copy-start | bytes 2359300
  213.9 5.7 %collective-permute-start.17 = (f32[128,1536]{1,0:T(8,128)S(1)}, f32[128,1536]{1,0:T(8,128)S(1)}, u32[]{:S(2)}, u32[]{:S(2)}) collective-permute-start(f32[128,1536]{1,0:T(8,128)S(1)} %get-tuple-element.49.refs_6_), channel_id=1, source_target_pairs={{0,32},{1,33},{2,34},{3,35},{4,36},{5,37},{6,38},{7,39},{8,40},{9,... | collective-permute-start | bytes 2359304 | tf_op jit(solution)/shard_map/ppermute | solution.py:292
  245.1 13.5 %all-to-all-start.7 = ((f32[32,8,128]{2,1,0:T(8,128)}), f32[32,8,128]{2,1,0:T(8,128)S(1)}, u32[]{:S(2)}, u32[]{:S(2)}) async-start(f32[32,8,128]{2,1,0:T(8,128)} %shard_map.83), calls=%async_computation.7 | async-start | bytes 262144 | tf_op jit(solution)/shard_map/all_to_all | solution.py:308
  249.5 12.7 %collective-permute-start.19 = (f32[128,128]{1,0:T(8,128)S(1)}, f32[128,128]{1,0:T(8,128)S(1)}, u32[]{:S(2)}, u32[]{:S(2)}) collective-permute-start(f32[128,128]{1,0:T(8,128)S(1)} %get-tuple-element.50), channel_id=1, source_target_pairs={{0,33},{1,34},{2,35},{3,36},{4,37},{5,38},{6,39},{7,40},{8,41},{9,... | collective-permute-start | bytes 196616 | tf_op jit(solution)/shard_map/ppermute | solution.py:292
  252.4 9.7 %collective-permute-start.20 = (f32[128,128]{1,0:T(8,128)S(1)}, f32[128,128]{1,0:T(8,128)S(1)}, u32[]{:S(2)}, u32[]{:S(2)}) collective-permute-start(f32[128,128]{1,0:T(8,128)S(1)} %get-tuple-element.51), channel_id=1, source_target_pairs={{0,63},{1,32},{2,33},{3,34},{4,35},{5,36},{6,37},{7,38},{8,39},{9,... | collective-permute-start | bytes 196616 | tf_op jit(solution)/shard_map/ppermute | solution.py:292
  258.7 9.0 %collective-permute-start.18 = (f32[2,16,8,128]{3,2,1,0:T(8,128)S(1)}, f32[2,16,8,128]{3,2,1,0:T(8,128)S(1)}, u32[]{:S(2)}, u32[]{:S(2)}) collective-permute-start(f32[2,16,8,128]{3,2,1,0:T(8,128)S(1)} %bitcast.44), channel_id=1, source_target_pairs={{0,32},{1,33},{2,34},{3,35},{4,36},{5,37},{6,38},{7,39},{8,40},{9,... | collective-permute-start | bytes 393224 | tf_op jit(solution)/shard_map/ppermute | solution.py:292
  267.6 13.5 %copy-start.5 = (bf16[12,384,256]{2,1,0:T(8,128)(2,1)S(1)}, bf16[12,384,256]{2,1,0:T(8,128)(2,1)}, u32[]{:S(2)}) copy-start(bf16[12,384,256]{2,1,0:T(8,128)(2,1)} %copy-done) | copy-start | bytes 7077892
  270.8 10.4 %collective-permute-start.21 = (f32[128,1536]{1,0:T(8,128)S(1)}, f32[128,1536]{1,0:T(8,128)S(1)}, u32[]{:S(2)}, u32[]{:S(2)}) collective-permute-start(f32[128,1536]{1,0:T(8,128)S(1)} %get-tuple-element.52), channel_id=1, source_target_pairs={{0,32},{1,33},{2,34},{3,35},{4,36},{5,37},{6,38},{7,39},{8,40},{9,... | collective-permute-start | bytes 2359304 | tf_op jit(solution)/shard_map/ppermute | solution.py:292
  270.8 7.1 %collective-permute-start.22 = (f32[128,128]{1,0:T(8,128)S(1)}, f32[128,128]{1,0:T(8,128)S(1)}, u32[]{:S(2)}, u32[]{:S(2)}) collective-permute-start(f32[128,128]{1,0:T(8,128)S(1)} %get-tuple-element.53), channel_id=1, source_target_pairs={{0,33},{1,34},{2,35},{3,36},{4,37},{5,38},{6,39},{7,40},{8,41},{9,... | collective-permute-start | bytes 196616 | tf_op jit(solution)/shard_map/ppermute | solution.py:292
  270.9 18.6 %copy-start.23 = (bf16[2,1536,256]{2,1,0:T(8,128)(2,1)S(1)}, bf16[2,1536,256]{2,1,0:T(8,128)(2,1)}, u32[]{:S(2)}) copy-start(bf16[2,1536,256]{2,1,0:T(8,128)(2,1)} %copy-done.19) | copy-start | bytes 4718596
  270.9 18.6 %copy-start.28 = (bf16[2,1536,256]{2,1,0:T(8,128)(2,1)S(1)}, bf16[2,1536,256]{2,1,0:T(8,128)(2,1)}, u32[]{:S(2)}) copy-start(bf16[2,1536,256]{2,1,0:T(8,128)(2,1)} %copy-done.24) | copy-start | bytes 4718596
  270.9 7.0 %collective-permute-start.23 = (f32[128,128]{1,0:T(8,128)S(1)}, f32[128,128]{1,0:T(8,128)S(1)}, u32[]{:S(2)}, u32[]{:S(2)}) collective-permute-start(f32[128,128]{1,0:T(8,128)S(1)} %get-tuple-element.54), channel_id=1, source_target_pairs={{0,63},{1,32},{2,33},{3,34},{4,35},{5,36},{6,37},{7,38},{8,39},{9,... | collective-permute-start | bytes 196616 | tf_op jit(solution)/shard_map/ppermute | solution.py:292
  283.8 5.7 %collective-permute-start.24 = (f32[128,1536]{1,0:T(8,128)S(1)}, f32[128,1536]{1,0:T(8,128)S(1)}, u32[]{:S(2)}, u32[]{:S(2)}) collective-permute-start(f32[128,1536]{1,0:T(8,128)S(1)} %get-tuple-element.55.refs_6_), channel_id=1, source_target_pairs={{0,32},{1,33},{2,34},{3,35},{4,36},{5,37},{6,38},{7,39},{8,40},{9,... | collective-permute-start | bytes 2359304 | tf_op jit(solution)/shard_map/ppermute | solution.py:292
  304.6 13.5 %all-to-all-start.9 = ((f32[32,8,128]{2,1,0:T(8,128)}), f32[32,8,128]{2,1,0:T(8,128)S(1)}, u32[]{:S(2)}, u32[]{:S(2)}) async-start(f32[32,8,128]{2,1,0:T(8,128)} %shard_map.88), calls=%async_computation.9 | async-start | bytes 262144 | tf_op jit(solution)/shard_map/all_to_all | solution.py:308
  308.9 12.7 %collective-permute-start.26 = (f32[128,128]{1,0:T(8,128)S(1)}, f32[128,128]{1,0:T(8,128)S(1)}, u32[]{:S(2)}, u32[]{:S(2)}) collective-permute-start(f32[128,128]{1,0:T(8,128)S(1)} %get-tuple-element.56), channel_id=1, source_target_pairs={{0,33},{1,34},{2,35},{3,36},{4,37},{5,38},{6,39},{7,40},{8,41},{9,... | collective-permute-start | bytes 196616 | tf_op jit(solution)/shard_map/ppermute | solution.py:292
  311.9 9.7 %collective-permute-start.27 = (f32[128,128]{1,0:T(8,128)S(1)}, f32[128,128]{1,0:T(8,128)S(1)}, u32[]{:S(2)}, u32[]{:S(2)}) collective-permute-start(f32[128,128]{1,0:T(8,128)S(1)} %get-tuple-element.57), channel_id=1, source_target_pairs={{0,63},{1,32},{2,33},{3,34},{4,35},{5,36},{6,37},{7,38},{8,39},{9,... | collective-permute-start | bytes 196616 | tf_op jit(solution)/shard_map/ppermute | solution.py:292
  318.1 9.0 %collective-permute-start.25 = (f32[2,16,8,128]{3,2,1,0:T(8,128)S(1)}, f32[2,16,8,128]{3,2,1,0:T(8,128)S(1)}, u32[]{:S(2)}, u32[]{:S(2)}) collective-permute-start(f32[2,16,8,128]{3,2,1,0:T(8,128)S(1)} %bitcast.42), channel_id=1, source_target_pairs={{0,32},{1,33},{2,34},{3,35},{4,36},{5,37},{6,38},{7,39},{8,40},{9,... | collective-permute-start | bytes 393224 | tf_op jit(solution)/shard_map/ppermute | solution.py:292
  (51 other events, 115.6 us)

commit v2 on v1

--- a/solution.py
+++ b/solution.py
@@ -8,7 +8,7 @@
 
 AXES = ("slab", "tile")
 BLOCK = 128
-PARAMS = pltpu.CompilerParams(vmem_limit_bytes=44 * 1024 * 1024)
+PARAMS = pltpu.CompilerParams(vmem_limit_bytes=24 * 1024 * 1024)
 SMEM = pl.BlockSpec(memory_space=pltpu.SMEM)
 
 
@@ -58,9 +58,9 @@
 
 def right_kernel(steps, count, flags, *refs):
     xs, (rh_ref, rl_ref, p_ref, acc) = refs[:count], refs[count:]
-    x = xs[0][...]
+    x = jnp.where(flags[0] == 1, 0.0, xs[0][...])
     if count == 2:
-        x = jnp.where(flags[3] == 1, xs[1][...], jnp.where(flags[0] == 1, 0.0, x))
+        x = jnp.where(flags[3] == 1, xs[1][...], x)
     high, low = halves(x)
     share = complex_dot(high, low, rh_ref[0], rl_ref[0], rh_ref[1], rl_ref[1])
 
@@ -69,8 +69,9 @@
 
     def finish():
         whole = acc[...]
-        p_ref[0] = whole[:, :BLOCK].reshape(p_ref.shape[1:])
-        p_ref[1] = whole[:, BLOCK:].reshape(p_ref.shape[1:])
+        half = p_ref.shape[0] // 2
+        p_ref[:half] = whole[:, :BLOCK].reshape(half, 8, BLOCK)
+        p_ref[half:] = whole[:, BLOCK:].reshape(half, 8, BLOCK)
 
     at_step(0, start)
 
@@ -81,25 +82,45 @@
     at_step(steps - 1, finish)
 
 
-def far_kernel(steps, count, pick, flags, *refs):
+def far_kernel(steps, count, flags, *refs):
     coefs, refs = refs[:count], refs[count:]
     weights, refs = refs[: 2 * count], refs[2 * count :]
-    bases, outs = (refs[:2], refs[2:]) if pick else (refs[:1], refs[1:])
-    base = bases[0][...]
-    if pick:
-        base = jnp.where(flags[3] == 1, bases[1][...], base)
-    total = base
+    if count == 2:
+        mh_ref, ml_ref, refs = refs[0], refs[1], refs[2:]
+    even_ref, odd_ref, t_ref, first_ref, last_ref = refs[:5]
+    scratch = refs[5:]
+
+    def flat(c_ref):
+        c = c_ref[...].reshape(2, -1, BLOCK)
+        return jnp.concatenate([c[0], c[1]], axis=1)
+
+    def load():
+        c = flat(coefs[0])
+        if count == 2:
+            other = flat(coefs[1])
+            high, low = halves(other)
+            scratch[2][...], scratch[3][...] = high, low
+            more = complex_dot(high, low, mh_ref[0], ml_ref[0], mh_ref[1], ml_ref[1])
+            c = c + jnp.where(flags[3] == 1, more, 0.0)
+        scratch[0][...], scratch[1][...] = halves(c)
+
+    at_step(0, load)
+    total = jnp.where(flags[3] == 1, odd_ref[...], even_ref[...])
     for k in range(count):
-        c_ref, high_ref, low_ref = coefs[k], weights[2 * k], weights[2 * k + 1]
-        c = jnp.concatenate([c_ref[0].reshape(-1, BLOCK), c_ref[1].reshape(-1, BLOCK)], axis=1)
-        high, low = halves(c)
+        high_ref, low_ref = weights[2 * k], weights[2 * k + 1]
+        high, low = scratch[2 * k][...], scratch[2 * k + 1][...]
         more = complex_dot(high, low, high_ref[0], low_ref[0], high_ref[1], low_ref[1])
         if k == 1:
             more = jnp.where(flags[3] == 1, more, 0.0)
         total = total + more
-    outs[0][...] = total
-    if len(outs) > 1:
-        store_edges(steps, total, *outs[1:])
+    t_ref[...] = total
+    store_edges(steps, total, first_ref, last_ref)
+
+
+def through_kernel(m_ref, high_ref, low_ref):
+    m = m_ref[...].reshape(2, -1, BLOCK)
+    m = jnp.concatenate([m[0], m[1]], axis=1)
+    high_ref[...], low_ref[...] = (part.reshape(high_ref.shape) for part in halves(m))
 
 
 def near_kernel(steps, group, own, edges, flags, x_ref, before_ref, after_ref, *refs):
@@ -166,6 +187,17 @@
     copies_ref[...] = jnp.broadcast_to(jnp.sum(parts_ref[...], axis=0)[None], copies_ref.shape)
 
 
+def join_kernel(sum_first, first_ref, second_ref, joined_ref):
+    depth = first_ref.shape[1]
+    first, second = first_ref[...], second_ref[...]
+    if sum_first:
+        first = jnp.broadcast_to(jnp.sum(first, axis=0)[None], first.shape)
+    else:
+        second = jnp.broadcast_to(jnp.sum(second, axis=0)[None], second.shape)
+    joined_ref[:, :depth] = first
+    joined_ref[:, depth:] = second
+
+
 def f32(*shape):
     return jax.ShapeDtypeStruct(shape, jnp.float32)
 
@@ -199,7 +231,7 @@
     steps = points // chunk
     trace = pl.BlockSpec((rows, chunk), lambda i: (0, i))
     right = pl.BlockSpec((2, chunk, rank), lambda i: (0, i, 0))
-    shape = (2, rows // 8, 8, BLOCK)
+    shape = (rows // 4, 8, BLOCK)
     return call(
         functools.partial(right_kernel, steps, len(xs)),
         (steps,),
@@ -212,28 +244,29 @@
     )
 
 
-def far_call(flags, coefs, weights, bases, edges):
+def far_call(flags, coefs, weights, through, bases, place=0):
     rows, points = bases[0].shape
     rank = weights[0].shape[1]
     chunk = chunk_of(points)
     steps = points // chunk
     trace = pl.BlockSpec((rows, chunk), lambda i: (0, i))
     left = pl.BlockSpec((2, rank, chunk), lambda i: (0, 0, i))
-    outs, shapes = [trace], [f32(rows, points)]
-    if edges:
-        outs, shapes = outs + [fixed(rows, BLOCK)] * 2, shapes + [f32(rows, BLOCK)] * 2
+    tiles = coefs[0].shape[0]
+    shape = (tiles, 2 * rows // tiles, BLOCK)
+    ins = [pl.BlockSpec(shape, lambda i, n=n: (0, n, 0)) for n in (place, 0)]
     return call(
-        functools.partial(far_kernel, steps, len(coefs), len(bases) == 2),
+        functools.partial(far_kernel, steps, len(coefs)),
         (steps,),
-        (flags, *coefs, *weights, *bases),
-        [SMEM, *[fixed(2, rows // 8, 8, BLOCK)] * len(coefs), *[left] * len(weights), *[trace] * len(bases)],
-        outs,
-        shapes,
+        (flags, *coefs, *weights, *through, *bases),
+        [SMEM, *ins[: len(coefs)], *[left] * len(weights), *[fixed(2, rank, rank)] * len(through), trace, trace],
+        [trace, fixed(rows, BLOCK), fixed(rows, BLOCK)],
+        [f32(rows, points), f32(rows, BLOCK), f32(rows, BLOCK)],
         len(coefs) * 3 * 4 * rows * points * rank,
-    )
-
-
-def near_call(flags, x, before, after, local, weights, edges):
+        [pltpu.VMEM((rows, rank), jnp.bfloat16)] * (2 * len(coefs)),
+    )
+
+
+def near_call(flags, x, before, after, local, weights, edges, place=0):
     rows, points = x.shape
     blocks, depth, width = weights[0].shape
     group = 4 if blocks % 4 == 0 else 1
@@ -241,6 +274,7 @@
     part = pl.BlockSpec((rows, group * BLOCK), lambda i: (0, i))
     near = pl.BlockSpec((group, depth, width), lambda i: (i, 0, 0))
     own = local is not None
+    edge = pl.BlockSpec((rows, BLOCK), lambda i: (place, 0))
     outs, shapes = [part], [f32(rows, points)]
     if edges:
         outs, shapes = outs + [fixed(rows, BLOCK)] * 2, shapes + [f32(rows, BLOCK)] * 2
@@ -248,7 +282,7 @@
         functools.partial(near_kernel, steps, group, own, edges),
         (steps,),
         (flags, x, before, after, *([local] if own else []), *weights),
-        [SMEM, fixed(rows, points), fixed(rows, BLOCK), fixed(rows, BLOCK), *([part] if own else []), near, near],
+        [SMEM, fixed(rows, points), edge, edge, *([part] if own else []), near, near],
         outs,
         shapes,
         3 * 2 * rows * blocks * depth * width,
@@ -259,7 +293,7 @@
 def split_left(x, factor):
     _, rank, points = x.shape
     part = pl.BlockSpec((1, rank, points), lambda i: (i, 0, 0))
-    shapes = [jax.ShapeDtypeStruct(x.shape, jnp.bfloat16)] * 2
+    shapes = [pltpu.VMEM(x.shape, jnp.bfloat16)] * 2
     if factor is None:
         return call(split_kernel, (2,), (x,), [part], [part] * 2, shapes)
     args = (x, factor.reshape(1, 1, points))
@@ -274,7 +308,7 @@
         pl.BlockSpec((group, 1, width), lambda i: (i, 0, 0)),
     ]
     out = pl.BlockSpec((group, depth, 2 * width), lambda i: (i, 0, 0))
-    shapes = [jax.ShapeDtypeStruct((blocks, depth, 2 * width), jnp.bfloat16)] * 2
+    shapes = [pltpu.VMEM((blocks, depth, 2 * width), jnp.bfloat16)] * 2
     return call(pair_kernel, (blocks // group,), (x, factor.reshape(blocks, 1, width)), ins, [out] * 2, shapes)
 
 
@@ -300,12 +334,27 @@
     def beside(x, across):
         return sent(x, lambda s: s, across)
 
-    def total(shares):
-        pieces = shares.reshape(tiles, -1, BLOCK)
-        parts = lax.all_to_all(pieces, "tile", 0, 0)
-        whole = lambda n: fixed(*n.shape)
-        copies = call(sum_kernel, (1,), (parts,), [whole(parts)], whole(parts), f32(*parts.shape))
-        return lax.all_to_all(copies, "tile", 0, 0).reshape(shares.shape)
+    def exchanged(pieces):
+        return lax.all_to_all(pieces, "tile", 0, 0)
+
+    def repeated(parts, place=0):
+        shape = (tiles, thin, BLOCK)
+        part = pl.BlockSpec(shape, lambda i: (0, place, 0))
+        return call(sum_kernel, (1,), (parts,), [part], fixed(*shape), f32(*shape))
+
+    def joined(sum_first, first, second):
+        shape = (tiles, thick + thin, BLOCK)
+        body = functools.partial(join_kernel, sum_first)
+        ins = [fixed(tiles, thick, BLOCK), fixed(tiles, thin, BLOCK)]
+        return call(body, (1,), (first, second), ins, fixed(*shape), f32(*shape))
+
+    def through_halves(both):
+        part = pl.BlockSpec((tiles, thick, BLOCK), lambda i: (0, 0, 0))
+        shapes = [pltpu.VMEM((2, rank, rank), jnp.bfloat16)] * 2
+        return call(through_kernel, (1,), (both,), [part], [fixed(2, rank, rank)] * 2, shapes)
+
+    thin = rows * rank // BLOCK // tiles
+    thick = 2 * rank * rank // BLOCK // tiles
 
     local = local_field[:, :, 0].reshape(rows, points)
     first, last = local[:, :BLOCK], local[:, points - BLOCK :]
@@ -313,33 +362,60 @@
         jnp.where(material[0][None, :] == jnp.arange(contrast.shape[0], dtype=jnp.int32)[:, None], contrast[:, None], 0.0),
         axis=0,
     )
+    tied = lax.optimization_barrier
+    w_arrived = partner(local)
+    lower, lower_factor = partner(low_left[0]), partner(factor)
     right = split_left(low_right[0], None)
-    left = split_left(low_left[0], factor)
-    near = split_near(near_blocks[0], factor)
-
-    w, w_first, w_last = local, first, last
-    arrived = jnp.zeros_like(local)
-    w_arrived = partner(w)
-    shares = right_call(flags, (arrived, w_arrived), right)
-    c = total(shares)
-    v = near_call(flags, w_arrived, partner(w_last, 1), partner(w_first, -1), local, near, False)[0]
-    t, first, last = far_call(flags, (c,), left, (w, v), True)
-
-    upper_flat = (partner(low_left[0]) * partner(factor)).reshape(2 * rank, points)
-    m = total(right_call(flags, (upper_flat,), right))
-    u_before = beside(upper_flat[:, points - BLOCK :], 1)
-    u_after = beside(upper_flat[:, :BLOCK], -1)
-    q = near_call(flags, upper_flat, u_before, u_after, None, near, False)[0]
-    g = far_call(flags, (m,), left, (q,), False)[0]
-    through = split_left(g.reshape(2, rank, points), None)
-
-    for _ in range(1, slabs // 2):
-        arrived = below(t)
-        w, w_first, w_last = near_call(flags, arrived, below(last, 1), below(first, -1), local, near, True)
-        w_arrived = partner(w)
-        c = total(right_call(flags, (arrived, w_arrived), right))
-        v = near_call(flags, w_arrived, partner(w_last, 1), partner(w_first, -1), local, near, False)[0]
-        t, first, last = far_call(flags, (c, partner(c)), (*left, *through), (w, v), True)
+
+    shares = right_call(flags, (w_arrived,), right)
+    shares, lower, left_in, here = tied((shares, lower, low_left[0], local))
+    parts = exchanged(shares)
+
+    def edge(start):
+        cut = slice(start, start + BLOCK)
+        return jnp.concatenate([(left_in[:, :, cut] * factor[cut]).reshape(2 * rank, BLOCK), here[:, cut]], axis=0)
+
+    before, after = partner(edge(points - BLOCK), 1), partner(edge(0), -1)
+    upper = (lower * lower_factor).reshape(2 * rank, points)
+    through_shares = right_call(flags, (upper,), right).reshape(tiles, thick, BLOCK)
+    parts, through_shares, before, after = tied((parts, through_shares, before, after))
+    pieces = joined(False, through_shares, parts)
+    pieces, upper, before, after, w_arrived, near_in = tied(
+        (pieces, upper, before, after, w_arrived, near_blocks[0])
+    )
+    both = exchanged(pieces)
+    near = split_near(near_in, factor)
+    v = near_call(flags, w_arrived, before, after, local, near, False, 2 * rank // rows)[0]
+    both, v, upper, before, after, left_in = tied((both, v, upper, before, after, low_left[0]))
+    left = split_left(left_in, factor)
+    t, first, last = far_call(flags, (both,), left, (), (local, v), thick // thin)
+    t, first, last, upper, upper_before, upper_after = tied((t, first, last, upper, before, after))
+
+    for step in range(1, slabs // 2):
+        arrived, before, after = below(t), below(last, 1), below(first, -1)
+        if step == 1:
+            q = near_call(flags, upper, upper_before, upper_after, None, near, False)[0]
+            across = split_left(q.reshape(2, rank, points), None)
+            before, after, across = tied((before, after, across))
+        w, w_first, w_last = near_call(flags, arrived, before, after, local, near, True)
+        w_arrived, w_before, w_after = partner(w), partner(w_last, 1), partner(w_first, -1)
+        shares = right_call(flags, (arrived, w_arrived), right)
+        if step == 1:
+            shares = joined(True, both, shares)
+            shares, across, w, w_arrived, w_before, w_after = tied((shares, across, w, w_arrived, w_before, w_after))
+        else:
+            shares, w, w_arrived, w_before, w_after = tied((shares, w, w_arrived, w_before, w_after))
+        parts = exchanged(shares)
+        copies = repeated(parts, thick // thin if step == 1 else 0)
+        if step == 1:
+            through = through_halves(parts)
+            copies, through, w, w_arrived, w_before, w_after = tied((copies, through, w, w_arrived, w_before, w_after))
+        else:
+            copies, w, w_arrived, w_before, w_after = tied((copies, w, w_arrived, w_before, w_after))
+        c = exchanged(copies)
+        c, w, w_arrived, w_before, w_after = tied((c, w, w_arrived, w_before, w_after))
+        v = near_call(flags, w_arrived, w_before, w_after, local, near, False)[0]
+        t, first, last = far_call(flags, (c, partner(c)), (*left, *across), through, (w, v))
     return t.reshape(2, sources, 1, points)
 
 

time: 338 us -> 274 us (0.81); the launches traced: 333 us -> 273 us
  blocking collectives: 53.3 us -> 97.5 us
  starting transfers between devices: 114 us -> 77.2 us
  waiting for transfers between devices: 55.2 us -> 18.7 us
  local copies, waits for them, and re-layouts: 45.2 us -> 16.7 us
  Pallas kernels: 61.7 us -> 56.6 us
  other arithmetic: 2.59 us -> 6.36 us
    all_to_all x3 -> x6, blocking collectives: 53.3 us -> 97.5 us  [exchanged(): return lax.all_to_all(pieces, 'tile', 0, 0)]
    unnamed x129 -> x33, local copies, waits for them, and re-layouts: 41.7 us -> 15 us
    all_to_all x7 -> x2, starting transfers between devices: 41.6 us -> 16.3 us  [exchanged(): return lax.all_to_all(pieces, 'tile', 0, 0)]
    all_to_all x7 -> x2, waiting for transfers between devices: 25.8 us -> 6.54 us  [exchanged(): return lax.all_to_all(pieces, 'tile', 0, 0)]
    ppermute x28 -> x26, waiting for transfers between devices: 29.4 us -> 12.1 us  [sent(): return lax.ppermute(x, AXES, pairs)]
    ppermute x28 -> x26, starting transfers between devices: 72.1 us -> 60.8 us  [sent(): return lax.ppermute(x, AXES, pairs)]
    pallas_call x27, Pallas kernels: 61.7 us -> 56.6 us  [call(): pl.pallas_call(body, grid=grid, in_specs=ins, out_specs=outs, out_shape=o...]
  transfers between devices with their start and end apart: 35 -> 28, of which waited for: 16 -> 7; matrix products, arithmetic and copies ran while one was open for 1% -> 3% of each run, Pallas kernels for 13% -> 13%
where the time goes in v2:
time: 274 us; the launch traced here: 273 us
  blocking collectives  97.5 us (36%)
  starting transfers between devices  77.2 us (28%)
  Pallas kernels  56.6 us (21%)
  waiting for transfers between devices  18.7 us (7%)
  local copies, waits for them, and re-layouts  16.7 us (6%)
  other arithmetic  6.36 us (2%)
    all_to_all x6, blocking collectives, exchanged(): return lax.all_to_all(pieces, 'tile', 0, 0)  97.5 us
    ppermute x26, starting transfers between devices, sent(): return lax.ppermute(x, AXES, pairs)  60.8 us
    pallas_call x27, Pallas kernels, call(): pl.pallas_call(body, grid=grid, in_specs=ins, out_specs=outs, out_shape=o...  56.6 us
    all_to_all x2, starting transfers between devices, exchanged(): return lax.all_to_all(pieces, 'tile', 0, 0)  16.3 us
    unnamed x33, local copies, waits for them, and re-layouts  15 us
    ppermute x26, waiting for transfers between devices, sent(): return lax.ppermute(x, AXES, pairs)  12.1 us
    all_to_all x2, waiting for transfers between devices, exchanged(): return lax.all_to_all(pieces, 'tile', 0, 0)  6.54 us
  transfers between devices with their start and end apart: 28, of which 7 were waited for; matrix products, arithmetic and copies ran while one was open for 3% of the time, Pallas kernels for 13%

profile of v2, /device:TPU:1, one launch (start us, length us, event | category | flops | bytes accessed | tf_op | source)
XLA Modules:
  0.0 273.5 jit_solution(1616613517005062454)
XLA Ops:
  0.0 3.2 %collective-permute-start.1 = (f32[2,256,1536]{2,1,0:T(8,128)}, f32[2,256,1536]{2,1,0:T(8,128)}, u32[]{:S(2)}, u32[]{:S(2)}) collective-permute-start(f32[2,256,1536]{2,1,0:T(8,128)} %bitcast.25), channel_id=1, source_target_pairs={{0,32},{1,33},{2,34},{3,35},{4,36},{5,37},{6,38},{7,39},{8,40},{9,... | collective-permute-start | bytes 9437192 | tf_op jit(solution)/shard_map/ppermute | solution.py:326
  9.7 2.6 shard_map.65
  13.5 9.3 %all-to-all-start = ((f32[32,8,128]{2,1,0:T(8,128)}), f32[32,8,128]{2,1,0:T(8,128)S(1)}, u32[]{:S(2)}, u32[]{:S(2)}) async-start(f32[32,8,128]{2,1,0:T(8,128)} %shard_map.65), calls=%async_computation | async-start | bytes 262144 | tf_op jit(solution)/shard_map/all_to_all | solution.py:338
  24.6 2.0 collective-permute-start.3
  27.5 3.4 %collective-permute-start.4 = (f32[640,128]{1,0:T(8,128)}, f32[640,128]{1,0:T(8,128)}, u32[]{:S(2)}, u32[]{:S(2)}) collective-permute-start(f32[640,128]{1,0:T(8,128)} %pad_maximum_fusion.1), channel_id=1, source_target_pairs={{0,63},{1,32},{2,33},{3,34},{4,35},{5,36},{6,37},{7,38},{8,39},{9,... | collective-permute-start | bytes 983048 | tf_op jit(solution)/shard_map/ppermute | solution.py:326
  30.9 2.2 broadcast_multiply_fusion
  33.1 4.0 %shard_map.66 = f32[128,8,128]{2,1,0:T(8,128)S(1)} custom-call(s32[4]{0:T(128)S(1)} %add_convert_fusion.flags, f32[512,1536]{1,0:T(8,128)S(1)} %bitcast.29, bf16[2,1536,256]{2,1,0:T(8,128)(2,1)S(1)} %get-tuple-element.113.refs_1_.refs_2_, bf16[2,1536,256]{2,1,0:T(8,128)(2,1)S(1)} %copy-done.5), custom_call_target="tpu_custom_call" | custom-call | flops 2415919104 | bytes 6291472 | tf_op jit(solution)/shard_map/pallas_call | solution.py:207
  40.2 7.0 %all-to-all-start.1 = ((f32[32,40,128]{2,1,0:T(8,128)}), f32[32,40,128]{2,1,0:T(8,128)}, u32[]{:S(2)}, u32[]{:S(2)}) async-start(f32[32,40,128]{2,1,0:T(8,128)} %shard_map.67), calls=%async_computation.1 | async-start | bytes 1310720 | tf_op jit(solution)/shard_map/all_to_all | solution.py:338
  47.3 2.3 copy-done.7
  52.2 3.0 %shard_map.69.refs_4_ = f32[128,1536]{1,0:T(8,128)S(1)} custom-call(s32[4]{0:T(128)S(1)} %add_convert_fusion.flags, f32[128,1536]{1,0:T(8,128)S(1)} %copy-done.10, f32[640,128]{1,0:T(8,128)} %collective-permute-done.3.before_ref, f32[640,128]{1,0:T(8,128)} %collective-permute-done.4.after_ref, f32[128,1536]{1,0:T(8,128)S(1)} %bitcast.16, ...), custom_call_target="tpu_custom_call" | custom-call | flops 905969664 | bytes 6946832 | tf_op jit(solution)/shard_map/pallas_call | solution.py:207
  57.5 6.5 %all-to-all-done.1.refs_0_.first_ref = f32[32,40,128]{2,1,0:T(8,128)} async-done(((f32[32,40,128]{2,1,0:T(8,128)}), f32[32,40,128]{2,1,0:T(8,128)}, u32[]{:S(2)}, u32[]{:S(2)}) %all-to-all-start.1) | async-done | bytes 655392 | tf_op jit(solution)/shard_map/all_to_all | solution.py:338
  68.0 2.4 shard_map.71
  70.4 5.0 %collective-permute-start.5 = (f32[128,1536]{1,0:T(8,128)S(1)}, f32[128,1536]{1,0:T(8,128)S(1)}, u32[]{:S(2)}, u32[]{:S(2)}) collective-permute-start(f32[128,1536]{1,0:T(8,128)S(1)} %get-tuple-element.142), channel_id=1, source_target_pairs={{0,32},{1,33},{2,34},{3,35},{4,36},{5,37},{6,38},{7,39},{8,40},{9,... | collective-permute-start | bytes 2359304 | tf_op jit(solution)/shard_map/ppermute | solution.py:326
  75.4 2.0 collective-permute-start.6
  77.4 4.1 %collective-permute-start.7 = (f32[128,128]{1,0:T(8,128)S(1)}, f32[128,128]{1,0:T(8,128)S(1)}, u32[]{:S(2)}, u32[]{:S(2)}) collective-permute-start(f32[128,128]{1,0:T(8,128)S(1)} %get-tuple-element.144), channel_id=1, source_target_pairs={{0,63},{1,32},{2,33},{3,34},{4,35},{5,36},{6,37},{7,38},{8,39},{9,... | collective-permute-start | bytes 196616 | tf_op jit(solution)/shard_map/ppermute | solution.py:326
  81.5 7.3 %shard_map.72 = f32[512,1536]{1,0:T(8,128)S(1)} custom-call(s32[4]{0:T(128)S(1)} %add_convert_fusion.flags, f32[512,1536]{1,0:T(8,128)S(1)} %bitcast.30, f32[640,128]{1,0:T(8,128)} %collective-permute-done.3.before_ref, f32[640,128]{1,0:T(8,128)} %collective-permute-done.4.after_ref, bf16[12,384,256]{2,1,0:T(8,128)(2,1)S(1)} %get-tuple-element.128.refs_1_.refs_0_, ...), custom_call_target="tpu_custom_call" | custom-call | flops 3623878656 | bytes 8519696 | tf_op jit(solution)/shard_map/pallas_call | solution.py:207
  89.4 2.6 shard_map.74
  93.1 4.1 %collective-permute-start.10 = (f32[128,128]{1,0:T(8,128)S(1)}, f32[128,128]{1,0:T(8,128)S(1)}, u32[]{:S(2)}, u32[]{:S(2)}) collective-permute-start(f32[128,128]{1,0:T(8,128)S(1)} %get-tuple-element.156), channel_id=1, source_target_pairs={{0,63},{1,32},{2,33},{3,34},{4,35},{5,36},{6,37},{7,38},{8,39},{9,... | collective-permute-start | bytes 196616 | tf_op jit(solution)/shard_map/ppermute | solution.py:326
  97.3 2.0 shard_map.75.second_ref
  100.5 22.1 %all_to_all.40.parts_ref.m_ref = f32[32,40,128]{2,1,0:T(8,128)S(1)} all-to-all(f32[32,40,128]{2,1,0:T(8,128)S(1)} %shard_map.76), channel_id=1, replica_groups=mesh['slab'=8,'tile'=32] {'tile'}, dimensions={0} | all-to-all | bytes 1310720 | tf_op jit(solution)/shard_map/all_to_all | solution.py:338
  122.7 17.2 %all_to_all.41.refs_0_ = f32[32,8,128]{2,1,0:T(8,128)S(1)} all-to-all(f32[32,8,128]{2,1,0:T(8,128)S(1)} %shard_map.77), channel_id=1, replica_groups=mesh['slab'=8,'tile'=32] {'tile'}, dimensions={0} | all-to-all | bytes 262144 | tf_op jit(solution)/shard_map/all_to_all | solution.py:338
  140.0 2.4 collective-permute-start.11
  142.3 2.6 shard_map.79.refs_9_
  144.9 3.2 %shard_map.80 = (f32[128,1536]{1,0:T(8,128)S(1)}, f32[128,128]{1,0:T(8,128)S(1)}, f32[128,128]{1,0:T(8,128)S(1)}) custom-call(s32[4]{0:T(128)S(1)} %add_convert_fusion.flags, f32[32,8,128]{2,1,0:T(8,128)S(1)} %all_to_all.41.refs_0_, f32[32,8,128]{2,1,0:T(8,128)S(1)} %collective-permute-done.11.refs_1_, ...), custom_call_target="tpu_custom_call" | custom-call | flops 1207959552 | bytes 8650768 | tf_op jit(solution)/shard_map/pallas_call | solution.py:207
  150.1 3.9 %collective-permute-start.14 = (f32[128,128]{1,0:T(8,128)S(1)}, f32[128,128]{1,0:T(8,128)S(1)}, u32[]{:S(2)}, u32[]{:S(2)}) collective-permute-start(f32[128,128]{1,0:T(8,128)S(1)} %get-tuple-element.180), channel_id=1, source_target_pairs={{0,63},{1,32},{2,33},{3,34},{4,35},{5,36},{6,37},{7,38},{8,39},{9,... | collective-permute-start | bytes 196616 | tf_op jit(solution)/shard_map/ppermute | solution.py:326
  154.0 2.7 collective-permute-done.13.before_ref
  156.7 2.7 collective-permute-done.12.x_ref.refs_0_
  159.4 2.6 shard_map.81
  162.0 2.9 %collective-permute-start.15 = (f32[128,1536]{1,0:T(8,128)S(1)}, f32[128,1536]{1,0:T(8,128)S(1)}, u32[]{:S(2)}, u32[]{:S(2)}) collective-permute-start(f32[128,1536]{1,0:T(8,128)S(1)} %get-tuple-element.195.refs_8_), channel_id=1, source_target_pairs={{0,32},{1,33},{2,34},{3,35},{4,36},{5,37},{6,38},{7,39},{8,40},{9,... | collective-permute-start | bytes 2359304 | tf_op jit(solution)/shard_map/ppermute | solution.py:326
  165.8 4.2 %collective-permute-start.17 = (f32[128,128]{1,0:T(8,128)S(1)}, f32[128,128]{1,0:T(8,128)S(1)}, u32[]{:S(2)}, u32[]{:S(2)}) collective-permute-start(f32[128,128]{1,0:T(8,128)S(1)} %get-tuple-element.183), channel_id=1, source_target_pairs={{0,63},{1,32},{2,33},{3,34},{4,35},{5,36},{6,37},{7,38},{8,39},{9,... | collective-permute-start | bytes 196616 | tf_op jit(solution)/shard_map/ppermute | solution.py:326
  170.0 2.0 shard_map.82
  172.0 15.7 %all_to_all.42.parts_ref = f32[32,8,128]{2,1,0:T(8,128)S(1)} all-to-all(f32[32,8,128]{2,1,0:T(8,128)S(1)} %shard_map.82), channel_id=1, replica_groups=mesh['slab'=8,'tile'=32] {'tile'}, dimensions={0} | all-to-all | bytes 262144 | tf_op jit(solution)/shard_map/all_to_all | solution.py:338
  187.8 13.3 %all_to_all.43.refs_0_ = f32[32,8,128]{2,1,0:T(8,128)S(1)} all-to-all(f32[32,8,128]{2,1,0:T(8,128)S(1)} %shard_map.83), channel_id=1, replica_groups=mesh['slab'=8,'tile'=32] {'tile'}, dimensions={0} | all-to-all | bytes 262144 | tf_op jit(solution)/shard_map/all_to_all | solution.py:338
  201.1 2.7 collective-permute-start.18
  203.8 2.6 shard_map.84.refs_9_
  206.5 3.2 %shard_map.85 = (f32[128,1536]{1,0:T(8,128)S(1)}, f32[128,128]{1,0:T(8,128)S(1)}, f32[128,128]{1,0:T(8,128)S(1)}) custom-call(s32[4]{0:T(128)S(1)} %add_convert_fusion.flags, f32[32,8,128]{2,1,0:T(8,128)S(1)} %all_to_all.43.refs_0_, f32[32,8,128]{2,1,0:T(8,128)S(1)} %collective-permute-done.18.refs_1_, ...), custom_call_target="tpu_custom_call" | custom-call | flops 1207959552 | bytes 8650768 | tf_op jit(solution)/shard_map/pallas_call | solution.py:207
  210.4 3.9 %collective-permute-start.21 = (f32[128,128]{1,0:T(8,128)S(1)}, f32[128,128]{1,0:T(8,128)S(1)}, u32[]{:S(2)}, u32[]{:S(2)}) collective-permute-start(f32[128,128]{1,0:T(8,128)S(1)} %get-tuple-element.201), channel_id=1, source_target_pairs={{0,63},{1,32},{2,33},{3,34},{4,35},{5,36},{6,37},{7,38},{8,39},{9,... | collective-permute-start | bytes 196616 | tf_op jit(solution)/shard_map/ppermute | solution.py:326
  214.3 2.4 collective-permute-done.20.before_ref
  216.8 3.2 %collective-permute-done.19.x_ref.refs_0_ = f32[128,1536]{1,0:T(8,128)S(1)} collective-permute-done((f32[128,1536]{1,0:T(8,128)S(1)}, f32[128,1536]{1,0:T(8,128)S(1)}, u32[]{:S(2)}, u32[]{:S(2)}) %collective-permute-start.19) | collective-permute-done | bytes 786464 | tf_op jit(solution)/shard_map/ppermute | solution.py:326
  220.0 2.6 shard_map.86
  222.6 3.8 %collective-permute-start.22 = (f32[128,1536]{1,0:T(8,128)S(1)}, f32[128,1536]{1,0:T(8,128)S(1)}, u32[]{:S(2)}, u32[]{:S(2)}) collective-permute-start(f32[128,1536]{1,0:T(8,128)S(1)} %get-tuple-element.216.refs_8_), channel_id=1, source_target_pairs={{0,32},{1,33},{2,34},{3,35},{4,36},{5,37},{6,38},{7,39},{8,40},{9,... | collective-permute-start | bytes 2359304 | tf_op jit(solution)/shard_map/ppermute | solution.py:326
  227.3 4.2 %collective-permute-start.24 = (f32[128,128]{1,0:T(8,128)S(1)}, f32[128,128]{1,0:T(8,128)S(1)}, u32[]{:S(2)}, u32[]{:S(2)}) collective-permute-start(f32[128,128]{1,0:T(8,128)S(1)} %get-tuple-element.204), channel_id=1, source_target_pairs={{0,63},{1,32},{2,33},{3,34},{4,35},{5,36},{6,37},{7,38},{8,39},{9,... | collective-permute-start | bytes 196616 | tf_op jit(solution)/shard_map/ppermute | solution.py:326
  231.5 2.0 shard_map.87
  233.6 15.7 %all_to_all.44.parts_ref = f32[32,8,128]{2,1,0:T(8,128)S(1)} all-to-all(f32[32,8,128]{2,1,0:T(8,128)S(1)} %shard_map.87), channel_id=1, replica_groups=mesh['slab'=8,'tile'=32] {'tile'}, dimensions={0} | all-to-all | bytes 262144 | tf_op jit(solution)/shard_map/all_to_all | solution.py:338
  249.3 13.3 %all_to_all.45.refs_0_ = f32[32,8,128]{2,1,0:T(8,128)S(1)} all-to-all(f32[32,8,128]{2,1,0:T(8,128)S(1)} %shard_map.88), channel_id=1, replica_groups=mesh['slab'=8,'tile'=32] {'tile'}, dimensions={0} | all-to-all | bytes 262144 | tf_op jit(solution)/shard_map/all_to_all | solution.py:338
  262.7 2.7 collective-permute-start.25
  265.4 2.6 shard_map.89.refs_9_
  268.0 3.8 %shard_map.90 = (f32[128,1536]{1,0:T(8,128)S(1)}, f32[128,128]{1,0:T(8,128)}, f32[128,128]{1,0:T(8,128)}) custom-call(s32[4]{0:T(128)S(1)} %add_convert_fusion.flags, f32[32,8,128]{2,1,0:T(8,128)S(1)} %all_to_all.45.refs_0_, f32[32,8,128]{2,1,0:T(8,128)S(1)} %collective-permute-done.25.refs_1_, bf16[2,256,1536]{2,1,0:T(8,128)(2,1)S(1)} %get-tuple-element.133.refs_1_.refs_2_, ...), custom_call_target="tpu_custom_call" | custom-call | flops 1207959552 | bytes 8650768 | tf_op jit(solution)/shard_map/pallas_call | solution.py:207
  (86 shorter events, 31.3 us)
Async XLA Ops:
  0.0 13.5 %collective-permute-start.1 = (f32[2,256,1536]{2,1,0:T(8,128)}, f32[2,256,1536]{2,1,0:T(8,128)}, u32[]{:S(2)}, u32[]{:S(2)}) collective-permute-start(f32[2,256,1536]{2,1,0:T(8,128)} %bitcast.25), channel_id=1, source_target_pairs={{0,32},{1,33},{2,34},{3,35},{4,36},{5,37},{6,38},{7,39},{8,40},{9,... | collective-permute-start | bytes 9437192 | tf_op jit(solution)/shard_map/ppermute | solution.py:326
  4.4 5.2 %collective-permute-start = (f32[128,1536]{1,0:T(8,128)S(1)}, f32[128,1536]{1,0:T(8,128)S(1)}, u32[]{:S(2)}, u32[]{:S(2)}) collective-permute-start(f32[128,1536]{1,0:T(8,128)S(1)} %bitcast.14), channel_id=1, source_target_pairs={{0,32},{1,33},{2,34},{3,35},{4,36},{5,37},{6,38},{7,39},{8,40},{9,... | collective-permute-start | bytes 2359304 | tf_op jit(solution)/shard_map/ppermute | solution.py:326
  6.0 24.9 %collective-permute-start.2 = (f32[1536]{0:T(1024)S(1)}, f32[1536]{0:T(1024)S(1)}, u32[]{:S(2)}, u32[]{:S(2)}) collective-permute-start(f32[1536]{0:T(1024)S(1)} %select_reduce_fusion), channel_id=1, source_target_pairs={{0,32},{1,33},{2,34},{3,35},{4,36},{5,37},{6,38},{7,39},{8,40},{9,... | collective-permute-start | bytes 18440 | tf_op jit(solution)/shard_map/ppermute | solution.py:326
  6.6 1.9 copy-start.11
  8.9 24.2 %copy-start.2 = (bf16[2,1536,256]{2,1,0:T(8,128)(2,1)}, bf16[2,1536,256]{2,1,0:T(8,128)(2,1)S(1)}, u32[]{:S(2)}) copy-start(bf16[2,1536,256]{2,1,0:T(8,128)(2,1)S(1)} %get-tuple-element.113.refs_1_.refs_2_) | copy-start | bytes 4718596
  9.7 15.0 %copy-start.9 = (f32[128,1536]{1,0:T(8,128)}, f32[128,1536]{1,0:T(8,128)S(1)}, u32[]{:S(2)}) copy-start(f32[128,1536]{1,0:T(8,128)S(1)} %collective-permute-done.refs_0_.x_ref) | copy-start | bytes 2359300
  12.3 1.2 copy-start.4
  13.5 25.3 %all-to-all-start = ((f32[32,8,128]{2,1,0:T(8,128)}), f32[32,8,128]{2,1,0:T(8,128)S(1)}, u32[]{:S(2)}, u32[]{:S(2)}) async-start(f32[32,8,128]{2,1,0:T(8,128)} %shard_map.65), calls=%async_computation | async-start | bytes 262144 | tf_op jit(solution)/shard_map/all_to_all | solution.py:338
  24.6 14.6 %collective-permute-start.3 = (f32[640,128]{1,0:T(8,128)}, f32[640,128]{1,0:T(8,128)}, u32[]{:S(2)}, u32[]{:S(2)}) collective-permute-start(f32[640,128]{1,0:T(8,128)} %pad_maximum_fusion), channel_id=1, source_target_pairs={{0,33},{1,34},{2,35},{3,36},{4,37},{5,38},{6,39},{7,40},{8,41},{9,... | collective-permute-start | bytes 983048 | tf_op jit(solution)/shard_map/ppermute | solution.py:326
  27.5 5.7 %copy-start.5 = (bf16[2,1536,256]{2,1,0:T(8,128)(2,1)S(1)}, bf16[2,1536,256]{2,1,0:T(8,128)(2,1)}, u32[]{:S(2)}) copy-start(bf16[2,1536,256]{2,1,0:T(8,128)(2,1)} %copy-done.4) | copy-start | bytes 4718596
  27.5 11.8 %collective-permute-start.4 = (f32[640,128]{1,0:T(8,128)}, f32[640,128]{1,0:T(8,128)}, u32[]{:S(2)}, u32[]{:S(2)}) collective-permute-start(f32[640,128]{1,0:T(8,128)} %pad_maximum_fusion.1), channel_id=1, source_target_pairs={{0,63},{1,32},{2,33},{3,34},{4,35},{5,36},{6,37},{7,38},{8,39},{9,... | collective-permute-start | bytes 983048 | tf_op jit(solution)/shard_map/ppermute | solution.py:326
  37.2 1.6 copy-start.12
  40.2 23.8 %all-to-all-start.1 = ((f32[32,40,128]{2,1,0:T(8,128)}), f32[32,40,128]{2,1,0:T(8,128)}, u32[]{:S(2)}, u32[]{:S(2)}) async-start(f32[32,40,128]{2,1,0:T(8,128)} %shard_map.67), calls=%async_computation.1 | async-start | bytes 1310720 | tf_op jit(solution)/shard_map/all_to_all | solution.py:338
  47.2 2.3 copy-start.7
  51.1 1.1 copy-start.10
  55.2 1.4 copy-start
  56.6 0.9 copy-start.14
  64.0 1.9 copy-start.8
  65.9 15.6 %copy-start.13 = (f32[2,256,1536]{2,1,0:T(8,128)S(1)}, f32[2,256,1536]{2,1,0:T(8,128)}, u32[]{:S(2)}) copy-start(f32[2,256,1536]{2,1,0:T(8,128)} %copy-done.12) | copy-start | bytes 9437188
  66.5 14.9 %copy-start.1 = (bf16[12,384,256]{2,1,0:T(8,128)(2,1)S(1)}, bf16[12,384,256]{2,1,0:T(8,128)(2,1)}, u32[]{:S(2)}) copy-start(bf16[12,384,256]{2,1,0:T(8,128)(2,1)} %copy-done) | copy-start | bytes 7077892
  66.5 1.4 copy-start.15
  70.4 18.9 %collective-permute-start.5 = (f32[128,1536]{1,0:T(8,128)S(1)}, f32[128,1536]{1,0:T(8,128)S(1)}, u32[]{:S(2)}, u32[]{:S(2)}) collective-permute-start(f32[128,1536]{1,0:T(8,128)S(1)} %get-tuple-element.142), channel_id=1, source_target_pairs={{0,32},{1,33},{2,34},{3,35},{4,36},{5,37},{6,38},{7,39},{8,40},{9,... | collective-permute-start | bytes 2359304 | tf_op jit(solution)/shard_map/ppermute | solution.py:326
  75.4 13.9 %collective-permute-start.6 = (f32[128,128]{1,0:T(8,128)S(1)}, f32[128,128]{1,0:T(8,128)S(1)}, u32[]{:S(2)}, u32[]{:S(2)}) collective-permute-start(f32[128,128]{1,0:T(8,128)S(1)} %get-tuple-element.143), channel_id=1, source_target_pairs={{0,33},{1,34},{2,35},{3,36},{4,37},{5,38},{6,39},{7,40},{8,41},{9,... | collective-permute-start | bytes 196616 | tf_op jit(solution)/shard_map/ppermute | solution.py:326
  77.4 11.9 %collective-permute-start.7 = (f32[128,128]{1,0:T(8,128)S(1)}, f32[128,128]{1,0:T(8,128)S(1)}, u32[]{:S(2)}, u32[]{:S(2)}) collective-permute-start(f32[128,128]{1,0:T(8,128)S(1)} %get-tuple-element.144), channel_id=1, source_target_pairs={{0,63},{1,32},{2,33},{3,34},{4,35},{5,36},{6,37},{7,38},{8,39},{9,... | collective-permute-start | bytes 196616 | tf_op jit(solution)/shard_map/ppermute | solution.py:326
  89.3 7.9 %copy-start.3 = (bf16[2,1536,256]{2,1,0:T(8,128)(2,1)S(1)}, bf16[2,1536,256]{2,1,0:T(8,128)(2,1)}, u32[]{:S(2)}) copy-start(bf16[2,1536,256]{2,1,0:T(8,128)(2,1)} %copy-done.2) | copy-start | bytes 4718596
  89.3 7.9 %copy-start.6 = (bf16[2,1536,256]{2,1,0:T(8,128)(2,1)S(1)}, bf16[2,1536,256]{2,1,0:T(8,128)(2,1)}, u32[]{:S(2)}) copy-start(bf16[2,1536,256]{2,1,0:T(8,128)(2,1)} %copy-done.4) | copy-start | bytes 4718596
  92.0 5.2 %collective-permute-start.8 = (f32[128,1536]{1,0:T(8,128)S(1)}, f32[128,1536]{1,0:T(8,128)S(1)}, u32[]{:S(2)}, u32[]{:S(2)}) collective-permute-start(f32[128,1536]{1,0:T(8,128)S(1)} %get-tuple-element.174.refs_8_), channel_id=1, source_target_pairs={{0,32},{1,33},{2,34},{3,35},{4,36},{5,37},{6,38},{7,39},{8,40},{9,... | collective-permute-start | bytes 2359304 | tf_op jit(solution)/shard_map/ppermute | solution.py:326
  92.1 8.3 %collective-permute-start.9 = (f32[128,128]{1,0:T(8,128)S(1)}, f32[128,128]{1,0:T(8,128)S(1)}, u32[]{:S(2)}, u32[]{:S(2)}) collective-permute-start(f32[128,128]{1,0:T(8,128)S(1)} %get-tuple-element.155), channel_id=1, source_target_pairs={{0,33},{1,34},{2,35},{3,36},{4,37},{5,38},{6,39},{7,40},{8,41},{9,... | collective-permute-start | bytes 196616 | tf_op jit(solution)/shard_map/ppermute | solution.py:326
  93.1 7.3 %collective-permute-start.10 = (f32[128,128]{1,0:T(8,128)S(1)}, f32[128,128]{1,0:T(8,128)S(1)}, u32[]{:S(2)}, u32[]{:S(2)}) collective-permute-start(f32[128,128]{1,0:T(8,128)S(1)} %get-tuple-element.156), channel_id=1, source_target_pairs={{0,63},{1,32},{2,33},{3,34},{4,35},{5,36},{6,37},{7,38},{8,39},{9,... | collective-permute-start | bytes 196616 | tf_op jit(solution)/shard_map/ppermute | solution.py:326
  140.0 5.0 %collective-permute-start.11 = (f32[32,8,128]{2,1,0:T(8,128)S(1)}, f32[32,8,128]{2,1,0:T(8,128)S(1)}, u32[]{:S(2)}, u32[]{:S(2)}) collective-permute-start(f32[32,8,128]{2,1,0:T(8,128)S(1)} %all_to_all.41.refs_0_), channel_id=1, source_target_pairs={{0,32},{1,33},{2,34},{3,35},{4,36},{5,37},{6,38},{7,39},{8,40},{9,... | collective-permute-start | bytes 393224 | tf_op jit(solution)/shard_map/ppermute | solution.py:326
  148.1 11.2 %collective-permute-start.12 = (f32[128,1536]{1,0:T(8,128)S(1)}, f32[128,1536]{1,0:T(8,128)S(1)}, u32[]{:S(2)}, u32[]{:S(2)}) collective-permute-start(f32[128,1536]{1,0:T(8,128)S(1)} %get-tuple-element.178), channel_id=1, source_target_pairs={{0,32},{1,33},{2,34},{3,35},{4,36},{5,37},{6,38},{7,39},{8,40},{9,... | collective-permute-start | bytes 2359304 | tf_op jit(solution)/shard_map/ppermute | solution.py:326
  149.0 7.7 %collective-permute-start.13 = (f32[128,128]{1,0:T(8,128)S(1)}, f32[128,128]{1,0:T(8,128)S(1)}, u32[]{:S(2)}, u32[]{:S(2)}) collective-permute-start(f32[128,128]{1,0:T(8,128)S(1)} %get-tuple-element.179), channel_id=1, source_target_pairs={{0,33},{1,34},{2,35},{3,36},{4,37},{5,38},{6,39},{7,40},{8,41},{9,... | collective-permute-start | bytes 196616 | tf_op jit(solution)/shard_map/ppermute | solution.py:326
  150.1 6.5 %collective-permute-start.14 = (f32[128,128]{1,0:T(8,128)S(1)}, f32[128,128]{1,0:T(8,128)S(1)}, u32[]{:S(2)}, u32[]{:S(2)}) collective-permute-start(f32[128,128]{1,0:T(8,128)S(1)} %get-tuple-element.180), channel_id=1, source_target_pairs={{0,63},{1,32},{2,33},{3,34},{4,35},{5,36},{6,37},{7,38},{8,39},{9,... | collective-permute-start | bytes 196616 | tf_op jit(solution)/shard_map/ppermute | solution.py:326
  162.0 8.0 %collective-permute-start.15 = (f32[128,1536]{1,0:T(8,128)S(1)}, f32[128,1536]{1,0:T(8,128)S(1)}, u32[]{:S(2)}, u32[]{:S(2)}) collective-permute-start(f32[128,1536]{1,0:T(8,128)S(1)} %get-tuple-element.195.refs_8_), channel_id=1, source_target_pairs={{0,32},{1,33},{2,34},{3,35},{4,36},{5,37},{6,38},{7,39},{8,40},{9,... | collective-permute-start | bytes 2359304 | tf_op jit(solution)/shard_map/ppermute | solution.py:326
  164.9 7.1 %collective-permute-start.16 = (f32[128,128]{1,0:T(8,128)S(1)}, f32[128,128]{1,0:T(8,128)S(1)}, u32[]{:S(2)}, u32[]{:S(2)}) collective-permute-start(f32[128,128]{1,0:T(8,128)S(1)} %get-tuple-element.182), channel_id=1, source_target_pairs={{0,33},{1,34},{2,35},{3,36},{4,37},{5,38},{6,39},{7,40},{8,41},{9,... | collective-permute-start | bytes 196616 | tf_op jit(solution)/shard_map/ppermute | solution.py:326
  165.8 6.3 %collective-permute-start.17 = (f32[128,128]{1,0:T(8,128)S(1)}, f32[128,128]{1,0:T(8,128)S(1)}, u32[]{:S(2)}, u32[]{:S(2)}) collective-permute-start(f32[128,128]{1,0:T(8,128)S(1)} %get-tuple-element.183), channel_id=1, source_target_pairs={{0,63},{1,32},{2,33},{3,34},{4,35},{5,36},{6,37},{7,38},{8,39},{9,... | collective-permute-start | bytes 196616 | tf_op jit(solution)/shard_map/ppermute | solution.py:326
  201.1 5.3 %collective-permute-start.18 = (f32[32,8,128]{2,1,0:T(8,128)S(1)}, f32[32,8,128]{2,1,0:T(8,128)S(1)}, u32[]{:S(2)}, u32[]{:S(2)}) collective-permute-start(f32[32,8,128]{2,1,0:T(8,128)S(1)} %all_to_all.43.refs_0_), channel_id=1, source_target_pairs={{0,32},{1,33},{2,34},{3,35},{4,36},{5,37},{6,38},{7,39},{8,40},{9,... | collective-permute-start | bytes 393224 | tf_op jit(solution)/shard_map/ppermute | solution.py:326
  209.7 10.4 %collective-permute-start.19 = (f32[128,1536]{1,0:T(8,128)S(1)}, f32[128,1536]{1,0:T(8,128)S(1)}, u32[]{:S(2)}, u32[]{:S(2)}) collective-permute-start(f32[128,1536]{1,0:T(8,128)S(1)} %get-tuple-element.199), channel_id=1, source_target_pairs={{0,32},{1,33},{2,34},{3,35},{4,36},{5,37},{6,38},{7,39},{8,40},{9,... | collective-permute-start | bytes 2359304 | tf_op jit(solution)/shard_map/ppermute | solution.py:326
  209.7 7.1 %collective-permute-start.20 = (f32[128,128]{1,0:T(8,128)S(1)}, f32[128,128]{1,0:T(8,128)S(1)}, u32[]{:S(2)}, u32[]{:S(2)}) collective-permute-start(f32[128,128]{1,0:T(8,128)S(1)} %get-tuple-element.200), channel_id=1, source_target_pairs={{0,33},{1,34},{2,35},{3,36},{4,37},{5,38},{6,39},{7,40},{8,41},{9,... | collective-permute-start | bytes 196616 | tf_op jit(solution)/shard_map/ppermute | solution.py:326
  210.4 6.3 %collective-permute-start.21 = (f32[128,128]{1,0:T(8,128)S(1)}, f32[128,128]{1,0:T(8,128)S(1)}, u32[]{:S(2)}, u32[]{:S(2)}) collective-permute-start(f32[128,128]{1,0:T(8,128)S(1)} %get-tuple-element.201), channel_id=1, source_target_pairs={{0,63},{1,32},{2,33},{3,34},{4,35},{5,36},{6,37},{7,38},{8,39},{9,... | collective-permute-start | bytes 196616 | tf_op jit(solution)/shard_map/ppermute | solution.py:326
  222.6 8.9 %collective-permute-start.22 = (f32[128,1536]{1,0:T(8,128)S(1)}, f32[128,1536]{1,0:T(8,128)S(1)}, u32[]{:S(2)}, u32[]{:S(2)}) collective-permute-start(f32[128,1536]{1,0:T(8,128)S(1)} %get-tuple-element.216.refs_8_), channel_id=1, source_target_pairs={{0,32},{1,33},{2,34},{3,35},{4,36},{5,37},{6,38},{7,39},{8,40},{9,... | collective-permute-start | bytes 2359304 | tf_op jit(solution)/shard_map/ppermute | solution.py:326
  226.4 7.1 %collective-permute-start.23 = (f32[128,128]{1,0:T(8,128)S(1)}, f32[128,128]{1,0:T(8,128)S(1)}, u32[]{:S(2)}, u32[]{:S(2)}) collective-permute-start(f32[128,128]{1,0:T(8,128)S(1)} %get-tuple-element.203), channel_id=1, source_target_pairs={{0,33},{1,34},{2,35},{3,36},{4,37},{5,38},{6,39},{7,40},{8,41},{9,... | collective-permute-start | bytes 196616 | tf_op jit(solution)/shard_map/ppermute | solution.py:326
  227.3 6.3 %collective-permute-start.24 = (f32[128,128]{1,0:T(8,128)S(1)}, f32[128,128]{1,0:T(8,128)S(1)}, u32[]{:S(2)}, u32[]{:S(2)}) collective-permute-start(f32[128,128]{1,0:T(8,128)S(1)} %get-tuple-element.204), channel_id=1, source_target_pairs={{0,63},{1,32},{2,33},{3,34},{4,35},{5,36},{6,37},{7,38},{8,39},{9,... | collective-permute-start | bytes 196616 | tf_op jit(solution)/shard_map/ppermute | solution.py:326
  262.7 5.3 %collective-permute-start.25 = (f32[32,8,128]{2,1,0:T(8,128)S(1)}, f32[32,8,128]{2,1,0:T(8,128)S(1)}, u32[]{:S(2)}, u32[]{:S(2)}) collective-permute-start(f32[32,8,128]{2,1,0:T(8,128)S(1)} %all_to_all.45.refs_0_), channel_id=1, source_target_pairs={{0,32},{1,33},{2,34},{3,35},{4,36},{5,37},{6,38},{7,39},{8,40},{9,... | collective-permute-start | bytes 393224 | tf_op jit(solution)/shard_map/ppermute | solution.py:326

commit v3 on v2

--- a/solution.py
+++ b/solution.py
@@ -56,9 +56,11 @@
     at_step(steps - 1, store_last)
 
 
-def right_kernel(steps, count, flags, *refs):
-    xs, (rh_ref, rl_ref, p_ref, acc) = refs[:count], refs[count:]
+def right_kernel(steps, count, scaled, flags, *refs):
+    xs, (rh_ref, rl_ref, p_ref, acc) = refs[:count], refs[-4:]
     x = jnp.where(flags[0] == 1, 0.0, xs[0][...])
+    if scaled:
+        x = x * refs[count][...]
     if count == 2:
         x = jnp.where(flags[3] == 1, xs[1][...], x)
     high, low = halves(x)
@@ -123,7 +125,9 @@
     high_ref[...], low_ref[...] = (part.reshape(high_ref.shape) for part in halves(m))
 
 
-def near_kernel(steps, group, own, edges, flags, x_ref, before_ref, after_ref, *refs):
+def near_kernel(steps, group, own, edges, scaled, flags, x_ref, before_ref, after_ref, *refs):
+    if scaled:
+        scale_ref, refs = refs[0], refs[1:]
     if own:
         l_ref, refs = refs[0], refs[1:]
     nh_ref, nl_ref, w_ref = refs[:3]
@@ -134,7 +138,8 @@
         before = jnp.where(flags[1] == 1, 0.0, before_ref[...])
         after = jnp.where(flags[2] == 1, 0.0, after_ref[...])
         high[:, :BLOCK], low[:, :BLOCK] = halves(before)
-        high[:, BLOCK : BLOCK + points], low[:, BLOCK : BLOCK + points] = halves(x_ref[...])
+        x = x_ref[...] * scale_ref[...] if scaled else x_ref[...]
+        high[:, BLOCK : BLOCK + points], low[:, BLOCK : BLOCK + points] = halves(x)
         high[:, BLOCK + points :], low[:, BLOCK + points :] = halves(after)
 
     at_step(0, load)
@@ -224,7 +229,7 @@
     return 512 if points % 512 == 0 else BLOCK
 
 
-def right_call(flags, xs, weights):
+def right_call(flags, xs, weights, scale=None):
     rows, points = xs[0].shape
     rank = weights[0].shape[2]
     chunk = chunk_of(points)
@@ -233,10 +238,16 @@
     right = pl.BlockSpec((2, chunk, rank), lambda i: (0, i, 0))
     shape = (rows // 4, 8, BLOCK)
     return call(
-        functools.partial(right_kernel, steps, len(xs)),
+        functools.partial(right_kernel, steps, len(xs), scale is not None),
         (steps,),
-        (flags, *xs, *weights),
-        [SMEM, *[trace] * len(xs), right, right],
+        (flags, *xs, *([] if scale is None else [scale]), *weights),
+        [
+            SMEM,
+            *[trace] * len(xs),
+            *([] if scale is None else [pl.BlockSpec((1, chunk), lambda i: (0, i))]),
+            right,
+            right,
+        ],
         fixed(*shape),
         f32(*shape),
         3 * 4 * rows * points * rank,
@@ -266,7 +277,7 @@
     )
 
 
-def near_call(flags, x, before, after, local, weights, edges, place=0):
+def near_call(flags, x, before, after, local, weights, edges, place=0, scale=None):
     rows, points = x.shape
     blocks, depth, width = weights[0].shape
     group = 4 if blocks % 4 == 0 else 1
@@ -279,10 +290,10 @@
     if edges:
         outs, shapes = outs + [fixed(rows, BLOCK)] * 2, shapes + [f32(rows, BLOCK)] * 2
     return call(
-        functools.partial(near_kernel, steps, group, own, edges),
+        functools.partial(near_kernel, steps, group, own, edges, scale is not None),
         (steps,),
-        (flags, x, before, after, *([local] if own else []), *weights),
-        [SMEM, fixed(rows, points), edge, edge, *([part] if own else []), near, near],
+        (flags, x, before, after, *([] if scale is None else [scale]), *([local] if own else []), *weights),
+        [SMEM, fixed(rows, points), edge, edge, *([] if scale is None else [fixed(1, points)]), *([part] if own else []), near, near],
         outs,
         shapes,
         3 * 2 * rows * blocks * depth * width,
@@ -290,10 +301,10 @@
     )
 
 
-def split_left(x, factor):
+def split_left(x, factor, held=True):
     _, rank, points = x.shape
     part = pl.BlockSpec((1, rank, points), lambda i: (i, 0, 0))
-    shapes = [pltpu.VMEM(x.shape, jnp.bfloat16)] * 2
+    shapes = [(pltpu.VMEM if held else jax.ShapeDtypeStruct)(x.shape, jnp.bfloat16)] * 2
     if factor is None:
         return call(split_kernel, (2,), (x,), [part], [part] * 2, shapes)
     args = (x, factor.reshape(1, 1, points))
@@ -376,8 +387,8 @@
         return jnp.concatenate([(left_in[:, :, cut] * factor[cut]).reshape(2 * rank, BLOCK), here[:, cut]], axis=0)
 
     before, after = partner(edge(points - BLOCK), 1), partner(edge(0), -1)
-    upper = (lower * lower_factor).reshape(2 * rank, points)
-    through_shares = right_call(flags, (upper,), right).reshape(tiles, thick, BLOCK)
+    upper, upper_scale = lower.reshape(2 * rank, points), lower_factor.reshape(1, points)
+    through_shares = right_call(flags, (upper,), right, upper_scale).reshape(tiles, thick, BLOCK)
     parts, through_shares, before, after = tied((parts, through_shares, before, after))
     pieces = joined(False, through_shares, parts)
     pieces, upper, before, after, w_arrived, near_in = tied(
@@ -386,17 +397,15 @@
     both = exchanged(pieces)
     near = split_near(near_in, factor)
     v = near_call(flags, w_arrived, before, after, local, near, False, 2 * rank // rows)[0]
-    both, v, upper, before, after, left_in = tied((both, v, upper, before, after, low_left[0]))
+    v, upper = tied((v, upper))
+    q = near_call(flags, upper, before, after, None, near, False, 0, upper_scale)[0]
+    across = split_left(q.reshape(2, rank, points), None, False)
+    both, v, across, left_in = tied((both, v, across, low_left[0]))
     left = split_left(left_in, factor)
     t, first, last = far_call(flags, (both,), left, (), (local, v), thick // thin)
-    t, first, last, upper, upper_before, upper_after = tied((t, first, last, upper, before, after))
 
     for step in range(1, slabs // 2):
         arrived, before, after = below(t), below(last, 1), below(first, -1)
-        if step == 1:
-            q = near_call(flags, upper, upper_before, upper_after, None, near, False)[0]
-            across = split_left(q.reshape(2, rank, points), None)
-            before, after, across = tied((before, after, across))
         w, w_first, w_last = near_call(flags, arrived, before, after, local, near, True)
         w_arrived, w_before, w_after = partner(w), partner(w_last, 1), partner(w_first, -1)
         shares = right_call(flags, (arrived, w_arrived), right)

time: 274 us -> 271 us (0.989)
  local copies, waits for them, and re-layouts: 16.7 us -> 13.3 us
  other arithmetic: 6.36 us -> 3.47 us
    all_to_all x2, waiting for transfers between devices: 6.54 us -> 1.6 us  [exchanged(): return lax.all_to_all(pieces, 'tile', 0, 0)]
    ppermute x26, waiting for transfers between devices: 12.1 us -> 16.7 us  [sent(): return lax.ppermute(x, AXES, pairs)]
    unnamed x33 -> x39, local copies, waits for them, and re-layouts: 15 us -> 11.5 us
    ppermute x26, starting transfers between devices: 60.8 us -> 63.9 us  [sent(): return lax.ppermute(x, AXES, pairs)]
  transfers between devices with their start and end apart: 28 -> 28, of which waited for: 7 -> 11; matrix products, arithmetic and copies ran while one was open for 3% -> 1% of each run, Pallas kernels for 13% -> 13%
where the time goes in v3:
time: 271 us; the launch traced here: 270 us
  blocking collectives  97.7 us (36%)
  starting transfers between devices  77.9 us (29%)
  Pallas kernels  58.6 us (22%)
  waiting for transfers between devices  18.3 us (7%)
  local copies, waits for them, and re-layouts  13.3 us (5%)
  other arithmetic  3.47 us (1%)
    all_to_all x6, blocking collectives, exchanged(): return lax.all_to_all(pieces, 'tile', 0, 0)  97.7 us
    ppermute x26, starting transfers between devices, sent(): return lax.ppermute(x, AXES, pairs)  63.9 us
    pallas_call x27, Pallas kernels, call(): pl.pallas_call(body, grid=grid, in_specs=ins, out_specs=outs, out_shape=o...  58.6 us
    ppermute x26, waiting for transfers between devices, sent(): return lax.ppermute(x, AXES, pairs)  16.7 us
    all_to_all x2, starting transfers between devices, exchanged(): return lax.all_to_all(pieces, 'tile', 0, 0)  14 us
    unnamed x39, local copies, waits for them, and re-layouts  11.5 us
  transfers between devices with their start and end apart: 28, of which 11 were waited for; matrix products, arithmetic and copies ran while one was open for 1% of the time, Pallas kernels for 13%

profile of v3, /device:TPU:1, one launch (start us, length us, event | category | flops | bytes accessed | tf_op | source)
XLA Modules:
  0.0 269.8 jit_solution(11223803203460282118)
XLA Ops:
  0.0 3.2 %collective-permute-start.1 = (f32[2,256,1536]{2,1,0:T(8,128)}, f32[2,256,1536]{2,1,0:T(8,128)}, u32[]{:S(2)}, u32[]{:S(2)}) collective-permute-start(f32[2,256,1536]{2,1,0:T(8,128)} %bitcast.25), channel_id=1, source_target_pairs={{0,32},{1,33},{2,34},{3,35},{4,36},{5,37},{6,38},{7,39},{8,40},{9,... | collective-permute-start | bytes 9437192 | tf_op jit(solution)/shard_map/ppermute | solution.py:337
  9.7 2.6 shard_map.65
  15.0 6.1 %collective-permute-start.4 = (f32[640,128]{1,0:T(8,128)}, f32[640,128]{1,0:T(8,128)}, u32[]{:S(2)}, u32[]{:S(2)}) collective-permute-start(f32[640,128]{1,0:T(8,128)} %pad_maximum_fusion.1), channel_id=1, source_target_pairs={{0,63},{1,32},{2,33},{3,34},{4,35},{5,36},{6,37},{7,38},{8,39},{9,... | collective-permute-start | bytes 983048 | tf_op jit(solution)/shard_map/ppermute | solution.py:337
  21.2 6.0 %all-to-all-start = ((f32[32,8,128]{2,1,0:T(8,128)}), f32[32,8,128]{2,1,0:T(8,128)S(1)}, u32[]{:S(2)}, u32[]{:S(2)}) async-start(f32[32,8,128]{2,1,0:T(8,128)} %shard_map.65), calls=%async_computation | async-start | bytes 262144 | tf_op jit(solution)/shard_map/all_to_all | solution.py:349
  30.1 4.6 %shard_map.66 = f32[128,8,128]{2,1,0:T(8,128)S(1)} custom-call(s32[4]{0:T(128)S(1)} %add_convert_fusion.flags, f32[512,1536]{1,0:T(8,128)} %bitcast.6.refs_0_.x_ref, f32[1,1536]{1,0:T(1,128)S(1)} %reshape.31.refs_1_.refs_0_, bf16[2,1536,256]{2,1,0:T(8,128)(2,1)S(1)} %get-tuple-element.104.refs_1_.refs_2_, bf16[2,1536,256]{2,1,0:T(8,128)(2,1)S(1)} %copy-done.5), custom_call_target="tpu_custom_call" | custom-call | flops 2415919104 | bytes 6297616 | tf_op jit(solution)/shard_map/pallas_call | solution.py:212
  37.3 8.0 %all-to-all-start.1 = ((f32[32,40,128]{2,1,0:T(8,128)}), f32[32,40,128]{2,1,0:T(8,128)}, u32[]{:S(2)}, u32[]{:S(2)}) async-start(f32[32,40,128]{2,1,0:T(8,128)} %shard_map.67), calls=%async_computation.1 | async-start | bytes 1310720 | tf_op jit(solution)/shard_map/all_to_all | solution.py:349
  45.4 2.3 copy-done.11
  49.2 3.0 %shard_map.69.refs_4_ = f32[128,1536]{1,0:T(8,128)S(1)} custom-call(s32[4]{0:T(128)S(1)} %add_convert_fusion.flags, f32[128,1536]{1,0:T(8,128)S(1)} %copy-done.14, f32[640,128]{1,0:T(8,128)S(1)} %collective-permute-done.3.before_ref, f32[640,128]{1,0:T(8,128)} %collective-permute-done.4.after_ref, f32[128,1536]{1,0:T(8,128)S(1)} %bitcast.16, ...), custom_call_target="tpu_custom_call" | custom-call | flops 905969664 | bytes 6946832 | tf_op jit(solution)/shard_map/pallas_call | solution.py:212
  52.3 8.6 %shard_map.70 = f32[512,1536]{1,0:T(8,128)S(1)} custom-call(s32[4]{0:T(128)S(1)} %add_convert_fusion.flags, f32[512,1536]{1,0:T(8,128)} %bitcast.6.refs_0_.x_ref, f32[640,128]{1,0:T(8,128)S(1)} %collective-permute-done.3.before_ref, f32[640,128]{1,0:T(8,128)} %collective-permute-done.4.after_ref, f32[1,1536]{1,0:T(1,128)S(1)} %reshape.31.refs_1_.refs_0_, ...), custom_call_target="tpu_custom_call" | custom-call | flops 3623878656 | bytes 8525840 | tf_op jit(solution)/shard_map/pallas_call | solution.py:212
  63.7 1.9 copy-done.12
  66.7 2.6 shard_map.73
  69.3 3.4 %collective-permute-start.5 = (f32[128,1536]{1,0:T(8,128)S(1)}, f32[128,1536]{1,0:T(8,128)S(1)}, u32[]{:S(2)}, u32[]{:S(2)}) collective-permute-start(f32[128,1536]{1,0:T(8,128)S(1)} %get-tuple-element.131), channel_id=1, source_target_pairs={{0,32},{1,33},{2,34},{3,35},{4,36},{5,37},{6,38},{7,39},{8,40},{9,... | collective-permute-start | bytes 2359304 | tf_op jit(solution)/shard_map/ppermute | solution.py:337
  72.7 2.0 collective-permute-start.6
  74.7 4.1 %collective-permute-start.7 = (f32[128,128]{1,0:T(8,128)S(1)}, f32[128,128]{1,0:T(8,128)S(1)}, u32[]{:S(2)}, u32[]{:S(2)}) collective-permute-start(f32[128,128]{1,0:T(8,128)S(1)} %get-tuple-element.133), channel_id=1, source_target_pairs={{0,63},{1,32},{2,33},{3,34},{4,35},{5,36},{6,37},{7,38},{8,39},{9,... | collective-permute-start | bytes 196616 | tf_op jit(solution)/shard_map/ppermute | solution.py:337
  80.1 2.9 %collective-permute-done.5.x_ref.refs_0_ = f32[128,1536]{1,0:T(8,128)S(1)} collective-permute-done((f32[128,1536]{1,0:T(8,128)S(1)}, f32[128,1536]{1,0:T(8,128)S(1)}, u32[]{:S(2)}, u32[]{:S(2)}) %collective-permute-start.5) | collective-permute-done | bytes 786464 | tf_op jit(solution)/shard_map/ppermute | solution.py:337
  83.0 2.6 shard_map.74
  85.7 2.6 collective-permute-start.8
  88.3 2.2 collective-permute-start.9
  90.4 2.9 %collective-permute-start.10 = (f32[128,128]{1,0:T(8,128)S(1)}, f32[128,128]{1,0:T(8,128)S(1)}, u32[]{:S(2)}, u32[]{:S(2)}) collective-permute-start(f32[128,128]{1,0:T(8,128)S(1)} %get-tuple-element.138), channel_id=1, source_target_pairs={{0,63},{1,32},{2,33},{3,34},{4,35},{5,36},{6,37},{7,38},{8,39},{9,... | collective-permute-start | bytes 196616 | tf_op jit(solution)/shard_map/ppermute | solution.py:337
  93.4 2.0 shard_map.75.second_ref
  96.6 22.2 %all_to_all.40.parts_ref.m_ref = f32[32,40,128]{2,1,0:T(8,128)S(1)} all-to-all(f32[32,40,128]{2,1,0:T(8,128)S(1)} %shard_map.76), channel_id=1, replica_groups=mesh['slab'=8,'tile'=32] {'tile'}, dimensions={0} | all-to-all | bytes 1310720 | tf_op jit(solution)/shard_map/all_to_all | solution.py:349
  118.9 17.3 %all_to_all.41.refs_0_ = f32[32,8,128]{2,1,0:T(8,128)S(1)} all-to-all(f32[32,8,128]{2,1,0:T(8,128)S(1)} %shard_map.77), channel_id=1, replica_groups=mesh['slab'=8,'tile'=32] {'tile'}, dimensions={0} | all-to-all | bytes 262144 | tf_op jit(solution)/shard_map/all_to_all | solution.py:349
  136.2 2.4 collective-permute-start.11
  138.6 2.6 shard_map.79.refs_9_
  141.3 3.2 %shard_map.80 = (f32[128,1536]{1,0:T(8,128)S(1)}, f32[128,128]{1,0:T(8,128)S(1)}, f32[128,128]{1,0:T(8,128)S(1)}) custom-call(s32[4]{0:T(128)S(1)} %add_convert_fusion.flags, f32[32,8,128]{2,1,0:T(8,128)S(1)} %all_to_all.41.refs_0_, f32[32,8,128]{2,1,0:T(8,128)S(1)} %collective-permute-done.11.refs_1_, ...), custom_call_target="tpu_custom_call" | custom-call | flops 1207959552 | bytes 8650768 | tf_op jit(solution)/shard_map/pallas_call | solution.py:212
  145.5 5.0 %collective-permute-start.14 = (f32[128,128]{1,0:T(8,128)S(1)}, f32[128,128]{1,0:T(8,128)S(1)}, u32[]{:S(2)}, u32[]{:S(2)}) collective-permute-start(f32[128,128]{1,0:T(8,128)S(1)} %get-tuple-element.162), channel_id=1, source_target_pairs={{0,63},{1,32},{2,33},{3,34},{4,35},{5,36},{6,37},{7,38},{8,39},{9,... | collective-permute-start | bytes 196616 | tf_op jit(solution)/shard_map/ppermute | solution.py:337
  151.9 2.9 %collective-permute-done.12.x_ref.refs_0_ = f32[128,1536]{1,0:T(8,128)S(1)} collective-permute-done((f32[128,1536]{1,0:T(8,128)S(1)}, f32[128,1536]{1,0:T(8,128)S(1)}, u32[]{:S(2)}, u32[]{:S(2)}) %collective-permute-start.12) | collective-permute-done | bytes 786464 | tf_op jit(solution)/shard_map/ppermute | solution.py:337
  154.8 2.6 shard_map.81
  157.4 3.8 %collective-permute-start.15 = (f32[128,1536]{1,0:T(8,128)S(1)}, f32[128,1536]{1,0:T(8,128)S(1)}, u32[]{:S(2)}, u32[]{:S(2)}) collective-permute-start(f32[128,1536]{1,0:T(8,128)S(1)} %get-tuple-element.177.refs_8_), channel_id=1, source_target_pairs={{0,32},{1,33},{2,34},{3,35},{4,36},{5,37},{6,38},{7,39},{8,40},{9,... | collective-permute-start | bytes 2359304 | tf_op jit(solution)/shard_map/ppermute | solution.py:337
  162.1 4.2 %collective-permute-start.17 = (f32[128,128]{1,0:T(8,128)S(1)}, f32[128,128]{1,0:T(8,128)S(1)}, u32[]{:S(2)}, u32[]{:S(2)}) collective-permute-start(f32[128,128]{1,0:T(8,128)S(1)} %get-tuple-element.165), channel_id=1, source_target_pairs={{0,63},{1,32},{2,33},{3,34},{4,35},{5,36},{6,37},{7,38},{8,39},{9,... | collective-permute-start | bytes 196616 | tf_op jit(solution)/shard_map/ppermute | solution.py:337
  166.3 2.0 shard_map.82
  168.3 15.7 %all_to_all.42.parts_ref = f32[32,8,128]{2,1,0:T(8,128)S(1)} all-to-all(f32[32,8,128]{2,1,0:T(8,128)S(1)} %shard_map.82), channel_id=1, replica_groups=mesh['slab'=8,'tile'=32] {'tile'}, dimensions={0} | all-to-all | bytes 262144 | tf_op jit(solution)/shard_map/all_to_all | solution.py:349
  184.1 13.3 %all_to_all.43.refs_0_ = f32[32,8,128]{2,1,0:T(8,128)S(1)} all-to-all(f32[32,8,128]{2,1,0:T(8,128)S(1)} %shard_map.83), channel_id=1, replica_groups=mesh['slab'=8,'tile'=32] {'tile'}, dimensions={0} | all-to-all | bytes 262144 | tf_op jit(solution)/shard_map/all_to_all | solution.py:349
  197.4 2.7 %collective-permute-start.18 = (f32[32,8,128]{2,1,0:T(8,128)S(1)}, f32[32,8,128]{2,1,0:T(8,128)S(1)}, u32[]{:S(2)}, u32[]{:S(2)}) collective-permute-start(f32[32,8,128]{2,1,0:T(8,128)S(1)} %all_to_all.43.refs_0_), channel_id=1, source_target_pairs={{0,32},{1,33},{2,34},{3,35},{4,36},{5,37},{6,38},{7,39},{8,40},{9,... | collective-permute-start | bytes 393224 | tf_op jit(solution)/shard_map/ppermute | solution.py:337
  200.2 2.6 shard_map.84.refs_9_
  202.8 3.2 %shard_map.85 = (f32[128,1536]{1,0:T(8,128)S(1)}, f32[128,128]{1,0:T(8,128)S(1)}, f32[128,128]{1,0:T(8,128)S(1)}) custom-call(s32[4]{0:T(128)S(1)} %add_convert_fusion.flags, f32[32,8,128]{2,1,0:T(8,128)S(1)} %all_to_all.43.refs_0_, f32[32,8,128]{2,1,0:T(8,128)S(1)} %collective-permute-done.18.refs_1_, ...), custom_call_target="tpu_custom_call" | custom-call | flops 1207959552 | bytes 8650768 | tf_op jit(solution)/shard_map/pallas_call | solution.py:212
  206.1 4.7 %collective-permute-start.21 = (f32[128,128]{1,0:T(8,128)S(1)}, f32[128,128]{1,0:T(8,128)S(1)}, u32[]{:S(2)}, u32[]{:S(2)}) collective-permute-start(f32[128,128]{1,0:T(8,128)S(1)} %get-tuple-element.183), channel_id=1, source_target_pairs={{0,63},{1,32},{2,33},{3,34},{4,35},{5,36},{6,37},{7,38},{8,39},{9,... | collective-permute-start | bytes 196616 | tf_op jit(solution)/shard_map/ppermute | solution.py:337
  210.8 2.3 collective-permute-done.20.before_ref
  213.1 3.2 %collective-permute-done.19.x_ref.refs_0_ = f32[128,1536]{1,0:T(8,128)S(1)} collective-permute-done((f32[128,1536]{1,0:T(8,128)S(1)}, f32[128,1536]{1,0:T(8,128)S(1)}, u32[]{:S(2)}, u32[]{:S(2)}) %collective-permute-start.19) | collective-permute-done | bytes 786464 | tf_op jit(solution)/shard_map/ppermute | solution.py:337
  216.3 2.6 shard_map.86
  219.0 3.8 %collective-permute-start.22 = (f32[128,1536]{1,0:T(8,128)S(1)}, f32[128,1536]{1,0:T(8,128)S(1)}, u32[]{:S(2)}, u32[]{:S(2)}) collective-permute-start(f32[128,1536]{1,0:T(8,128)S(1)} %get-tuple-element.198.refs_8_), channel_id=1, source_target_pairs={{0,32},{1,33},{2,34},{3,35},{4,36},{5,37},{6,38},{7,39},{8,40},{9,... | collective-permute-start | bytes 2359304 | tf_op jit(solution)/shard_map/ppermute | solution.py:337
  223.6 4.2 %collective-permute-start.24 = (f32[128,128]{1,0:T(8,128)S(1)}, f32[128,128]{1,0:T(8,128)S(1)}, u32[]{:S(2)}, u32[]{:S(2)}) collective-permute-start(f32[128,128]{1,0:T(8,128)S(1)} %get-tuple-element.186), channel_id=1, source_target_pairs={{0,63},{1,32},{2,33},{3,34},{4,35},{5,36},{6,37},{7,38},{8,39},{9,... | collective-permute-start | bytes 196616 | tf_op jit(solution)/shard_map/ppermute | solution.py:337
  227.8 2.0 shard_map.87
  229.9 15.7 %all_to_all.44.parts_ref = f32[32,8,128]{2,1,0:T(8,128)S(1)} all-to-all(f32[32,8,128]{2,1,0:T(8,128)S(1)} %shard_map.87), channel_id=1, replica_groups=mesh['slab'=8,'tile'=32] {'tile'}, dimensions={0} | all-to-all | bytes 262144 | tf_op jit(solution)/shard_map/all_to_all | solution.py:349
  245.6 13.3 %all_to_all.45.refs_0_ = f32[32,8,128]{2,1,0:T(8,128)S(1)} all-to-all(f32[32,8,128]{2,1,0:T(8,128)S(1)} %shard_map.88), channel_id=1, replica_groups=mesh['slab'=8,'tile'=32] {'tile'}, dimensions={0} | all-to-all | bytes 262144 | tf_op jit(solution)/shard_map/all_to_all | solution.py:349
  259.0 2.7 %collective-permute-start.25 = (f32[32,8,128]{2,1,0:T(8,128)S(1)}, f32[32,8,128]{2,1,0:T(8,128)S(1)}, u32[]{:S(2)}, u32[]{:S(2)}) collective-permute-start(f32[32,8,128]{2,1,0:T(8,128)S(1)} %all_to_all.45.refs_0_), channel_id=1, source_target_pairs={{0,32},{1,33},{2,34},{3,35},{4,36},{5,37},{6,38},{7,39},{8,40},{9,... | collective-permute-start | bytes 393224 | tf_op jit(solution)/shard_map/ppermute | solution.py:337
  261.7 2.6 shard_map.89.refs_9_
  264.3 3.8 %shard_map.90 = (f32[128,1536]{1,0:T(8,128)S(1)}, f32[128,128]{1,0:T(8,128)}, f32[128,128]{1,0:T(8,128)}) custom-call(s32[4]{0:T(128)S(1)} %add_convert_fusion.flags, f32[32,8,128]{2,1,0:T(8,128)S(1)} %all_to_all.45.refs_0_, f32[32,8,128]{2,1,0:T(8,128)S(1)} %collective-permute-done.25.refs_1_, bf16[2,256,1536]{2,1,0:T(8,128)(2,1)S(1)} %get-tuple-element.128.refs_1_.refs_2_, ...), custom_call_target="tpu_custom_call" | custom-call | flops 1207959552 | bytes 8650768 | tf_op jit(solution)/shard_map/pallas_call | solution.py:212
  (92 shorter events, 28.8 us)
Async XLA Ops:
  0.0 7.7 %copy-start.18 = (f32[16]{0:T(128)S(1)}, f32[16]{0:T(128)}, u32[]{:S(2)}) copy-start(f32[16]{0:T(128)} %param.8) | copy-start | bytes 196
  0.0 12.3 %collective-permute-start.1 = (f32[2,256,1536]{2,1,0:T(8,128)}, f32[2,256,1536]{2,1,0:T(8,128)}, u32[]{:S(2)}, u32[]{:S(2)}) collective-permute-start(f32[2,256,1536]{2,1,0:T(8,128)} %bitcast.25), channel_id=1, source_target_pairs={{0,32},{1,33},{2,34},{3,35},{4,36},{5,37},{6,38},{7,39},{8,40},{9,... | collective-permute-start | bytes 9437192 | tf_op jit(solution)/shard_map/ppermute | solution.py:337
  4.4 5.2 %collective-permute-start = (f32[128,1536]{1,0:T(8,128)S(1)}, f32[128,1536]{1,0:T(8,128)S(1)}, u32[]{:S(2)}, u32[]{:S(2)}) collective-permute-start(f32[128,1536]{1,0:T(8,128)S(1)} %bitcast.14), channel_id=1, source_target_pairs={{0,32},{1,33},{2,34},{3,35},{4,36},{5,37},{6,38},{7,39},{8,40},{9,... | collective-permute-start | bytes 2359304 | tf_op jit(solution)/shard_map/ppermute | solution.py:337
  5.3 1.9 copy-start.15
  7.6 5.8 %copy-start.4 = (bf16[2,1536,256]{2,1,0:T(8,128)(2,1)}, bf16[2,1536,256]{2,1,0:T(8,128)(2,1)S(1)}, u32[]{:S(2)}) copy-start(bf16[2,1536,256]{2,1,0:T(8,128)(2,1)S(1)} %get-tuple-element.105.refs_2_.refs_3_) | copy-start | bytes 4718596
  7.6 21.1 %copy-start.2 = (bf16[2,1536,256]{2,1,0:T(8,128)(2,1)}, bf16[2,1536,256]{2,1,0:T(8,128)(2,1)S(1)}, u32[]{:S(2)}) copy-start(bf16[2,1536,256]{2,1,0:T(8,128)(2,1)S(1)} %get-tuple-element.104.refs_1_.refs_2_) | copy-start | bytes 4718596
  9.7 3.7 %copy-start.13 = (f32[128,1536]{1,0:T(8,128)}, f32[128,1536]{1,0:T(8,128)S(1)}, u32[]{:S(2)}) copy-start(f32[128,1536]{1,0:T(8,128)S(1)} %collective-permute-done.refs_0_.x_ref) | copy-start | bytes 2359300
  14.1 22.2 %collective-permute-start.3 = (f32[640,128]{1,0:T(8,128)}, f32[640,128]{1,0:T(8,128)S(1)}, u32[]{:S(2)}, u32[]{:S(2)}) collective-permute-start(f32[640,128]{1,0:T(8,128)} %pad_maximum_fusion), channel_id=1, source_target_pairs={{0,33},{1,34},{2,35},{3,36},{4,37},{5,38},{6,39},{7,40},{8,41},{9,... | collective-permute-start | bytes 983048 | tf_op jit(solution)/shard_map/ppermute | solution.py:337
  15.0 21.3 %collective-permute-start.4 = (f32[640,128]{1,0:T(8,128)}, f32[640,128]{1,0:T(8,128)}, u32[]{:S(2)}, u32[]{:S(2)}) collective-permute-start(f32[640,128]{1,0:T(8,128)} %pad_maximum_fusion.1), channel_id=1, source_target_pairs={{0,63},{1,32},{2,33},{3,34},{4,35},{5,36},{6,37},{7,38},{8,39},{9,... | collective-permute-start | bytes 983048 | tf_op jit(solution)/shard_map/ppermute | solution.py:337
  21.2 15.1 %all-to-all-start = ((f32[32,8,128]{2,1,0:T(8,128)}), f32[32,8,128]{2,1,0:T(8,128)S(1)}, u32[]{:S(2)}, u32[]{:S(2)}) async-start(f32[32,8,128]{2,1,0:T(8,128)} %shard_map.65), calls=%async_computation | async-start | bytes 262144 | tf_op jit(solution)/shard_map/all_to_all | solution.py:349
  27.2 1.6 collective-permute-start.2
  28.7 1.4 copy-start.5
  37.3 26.4 %all-to-all-start.1 = ((f32[32,40,128]{2,1,0:T(8,128)}), f32[32,40,128]{2,1,0:T(8,128)}, u32[]{:S(2)}, u32[]{:S(2)}) async-start(f32[32,40,128]{2,1,0:T(8,128)} %shard_map.67), calls=%async_computation.1 | async-start | bytes 1310720 | tf_op jit(solution)/shard_map/all_to_all | solution.py:349
  45.4 2.3 copy-start.11
  47.7 1.5 copy-start.14
  49.2 3.1 %copy-start = (bf16[12,384,256]{2,1,0:T(8,128)(2,1)}, bf16[12,384,256]{2,1,0:T(8,128)(2,1)S(1)}, u32[]{:S(2)}) copy-start(bf16[12,384,256]{2,1,0:T(8,128)(2,1)S(1)} %get-tuple-element.120.refs_2_) | copy-start | bytes 7077892
  52.3 8.6 %copy-start.16 = (f32[128,1536]{1,0:T(8,128)}, f32[128,1536]{1,0:T(8,128)S(1)}, u32[]{:S(2)}) copy-start(f32[128,1536]{1,0:T(8,128)S(1)} %shard_map.69.refs_4_) | copy-start | bytes 2359300
  61.4 1.2 copy-start.7
  62.6 1.1 copy-start.9
  63.7 1.9 copy-start.12
  65.6 1.1 copy-start.17
  66.7 16.3 %copy-start.1 = (bf16[12,384,256]{2,1,0:T(8,128)(2,1)S(1)}, bf16[12,384,256]{2,1,0:T(8,128)(2,1)}, u32[]{:S(2)}) copy-start(bf16[12,384,256]{2,1,0:T(8,128)(2,1)} %copy-done) | copy-start | bytes 7077892
  69.3 13.7 %collective-permute-start.5 = (f32[128,1536]{1,0:T(8,128)S(1)}, f32[128,1536]{1,0:T(8,128)S(1)}, u32[]{:S(2)}, u32[]{:S(2)}) collective-permute-start(f32[128,1536]{1,0:T(8,128)S(1)} %get-tuple-element.131), channel_id=1, source_target_pairs={{0,32},{1,33},{2,34},{3,35},{4,36},{5,37},{6,38},{7,39},{8,40},{9,... | collective-permute-start | bytes 2359304 | tf_op jit(solution)/shard_map/ppermute | solution.py:337
  72.7 7.3 %collective-permute-start.6 = (f32[128,128]{1,0:T(8,128)S(1)}, f32[128,128]{1,0:T(8,128)S(1)}, u32[]{:S(2)}, u32[]{:S(2)}) collective-permute-start(f32[128,128]{1,0:T(8,128)S(1)} %get-tuple-element.132), channel_id=1, source_target_pairs={{0,33},{1,34},{2,35},{3,36},{4,37},{5,38},{6,39},{7,40},{8,41},{9,... | collective-permute-start | bytes 196616 | tf_op jit(solution)/shard_map/ppermute | solution.py:337
  74.7 18.7 %copy-start.3 = (bf16[2,1536,256]{2,1,0:T(8,128)(2,1)S(1)}, bf16[2,1536,256]{2,1,0:T(8,128)(2,1)}, u32[]{:S(2)}) copy-start(bf16[2,1536,256]{2,1,0:T(8,128)(2,1)} %copy-done.2) | copy-start | bytes 4718596
  74.7 18.7 %copy-start.6 = (bf16[2,1536,256]{2,1,0:T(8,128)(2,1)S(1)}, bf16[2,1536,256]{2,1,0:T(8,128)(2,1)}, u32[]{:S(2)}) copy-start(bf16[2,1536,256]{2,1,0:T(8,128)(2,1)} %copy-done.4) | copy-start | bytes 4718596
  74.7 5.4 %collective-permute-start.7 = (f32[128,128]{1,0:T(8,128)S(1)}, f32[128,128]{1,0:T(8,128)S(1)}, u32[]{:S(2)}, u32[]{:S(2)}) collective-permute-start(f32[128,128]{1,0:T(8,128)S(1)} %get-tuple-element.133), channel_id=1, source_target_pairs={{0,63},{1,32},{2,33},{3,34},{4,35},{5,36},{6,37},{7,38},{8,39},{9,... | collective-permute-start | bytes 196616 | tf_op jit(solution)/shard_map/ppermute | solution.py:337
  85.7 7.7 %collective-permute-start.8 = (f32[128,1536]{1,0:T(8,128)S(1)}, f32[128,1536]{1,0:T(8,128)S(1)}, u32[]{:S(2)}, u32[]{:S(2)}) collective-permute-start(f32[128,1536]{1,0:T(8,128)S(1)} %get-tuple-element.156.refs_8_), channel_id=1, source_target_pairs={{0,32},{1,33},{2,34},{3,35},{4,36},{5,37},{6,38},{7,39},{8,40},{9,... | collective-permute-start | bytes 2359304 | tf_op jit(solution)/shard_map/ppermute | solution.py:337
  88.3 8.3 %collective-permute-start.9 = (f32[128,128]{1,0:T(8,128)S(1)}, f32[128,128]{1,0:T(8,128)S(1)}, u32[]{:S(2)}, u32[]{:S(2)}) collective-permute-start(f32[128,128]{1,0:T(8,128)S(1)} %get-tuple-element.137), channel_id=1, source_target_pairs={{0,33},{1,34},{2,35},{3,36},{4,37},{5,38},{6,39},{7,40},{8,41},{9,... | collective-permute-start | bytes 196616 | tf_op jit(solution)/shard_map/ppermute | solution.py:337
  90.4 6.1 %collective-permute-start.10 = (f32[128,128]{1,0:T(8,128)S(1)}, f32[128,128]{1,0:T(8,128)S(1)}, u32[]{:S(2)}, u32[]{:S(2)}) collective-permute-start(f32[128,128]{1,0:T(8,128)S(1)} %get-tuple-element.138), channel_id=1, source_target_pairs={{0,63},{1,32},{2,33},{3,34},{4,35},{5,36},{6,37},{7,38},{8,39},{9,... | collective-permute-start | bytes 196616 | tf_op jit(solution)/shard_map/ppermute | solution.py:337
  136.2 5.0 %copy-start.8 = (bf16[2,256,1536]{2,1,0:T(8,128)(2,1)S(1)}, bf16[2,256,1536]{2,1,0:T(8,128)(2,1)}, u32[]{:S(2)}) copy-start(bf16[2,256,1536]{2,1,0:T(8,128)(2,1)} %copy-done.7) | copy-start | bytes 4718596
  136.2 5.0 %copy-start.10 = (bf16[2,256,1536]{2,1,0:T(8,128)(2,1)S(1)}, bf16[2,256,1536]{2,1,0:T(8,128)(2,1)}, u32[]{:S(2)}) copy-start(bf16[2,256,1536]{2,1,0:T(8,128)(2,1)} %copy-done.9) | copy-start | bytes 4718596
  136.2 5.0 %collective-permute-start.11 = (f32[32,8,128]{2,1,0:T(8,128)S(1)}, f32[32,8,128]{2,1,0:T(8,128)S(1)}, u32[]{:S(2)}, u32[]{:S(2)}) collective-permute-start(f32[32,8,128]{2,1,0:T(8,128)S(1)} %all_to_all.41.refs_0_), channel_id=1, source_target_pairs={{0,32},{1,33},{2,34},{3,35},{4,36},{5,37},{6,38},{7,39},{8,40},{9,... | collective-permute-start | bytes 393224 | tf_op jit(solution)/shard_map/ppermute | solution.py:337
  144.4 10.4 %collective-permute-start.12 = (f32[128,1536]{1,0:T(8,128)S(1)}, f32[128,1536]{1,0:T(8,128)S(1)}, u32[]{:S(2)}, u32[]{:S(2)}) collective-permute-start(f32[128,1536]{1,0:T(8,128)S(1)} %get-tuple-element.160), channel_id=1, source_target_pairs={{0,32},{1,33},{2,34},{3,35},{4,36},{5,37},{6,38},{7,39},{8,40},{9,... | collective-permute-start | bytes 2359304 | tf_op jit(solution)/shard_map/ppermute | solution.py:337
  144.5 7.3 %collective-permute-start.13 = (f32[128,128]{1,0:T(8,128)S(1)}, f32[128,128]{1,0:T(8,128)S(1)}, u32[]{:S(2)}, u32[]{:S(2)}) collective-permute-start(f32[128,128]{1,0:T(8,128)S(1)} %get-tuple-element.161), channel_id=1, source_target_pairs={{0,33},{1,34},{2,35},{3,36},{4,37},{5,38},{6,39},{7,40},{8,41},{9,... | collective-permute-start | bytes 196616 | tf_op jit(solution)/shard_map/ppermute | solution.py:337
  145.5 6.4 %collective-permute-start.14 = (f32[128,128]{1,0:T(8,128)S(1)}, f32[128,128]{1,0:T(8,128)S(1)}, u32[]{:S(2)}, u32[]{:S(2)}) collective-permute-start(f32[128,128]{1,0:T(8,128)S(1)} %get-tuple-element.162), channel_id=1, source_target_pairs={{0,63},{1,32},{2,33},{3,34},{4,35},{5,36},{6,37},{7,38},{8,39},{9,... | collective-permute-start | bytes 196616 | tf_op jit(solution)/shard_map/ppermute | solution.py:337
  157.4 8.9 %collective-permute-start.15 = (f32[128,1536]{1,0:T(8,128)S(1)}, f32[128,1536]{1,0:T(8,128)S(1)}, u32[]{:S(2)}, u32[]{:S(2)}) collective-permute-start(f32[128,1536]{1,0:T(8,128)S(1)} %get-tuple-element.177.refs_8_), channel_id=1, source_target_pairs={{0,32},{1,33},{2,34},{3,35},{4,36},{5,37},{6,38},{7,39},{8,40},{9,... | collective-permute-start | bytes 2359304 | tf_op jit(solution)/shard_map/ppermute | solution.py:337
  161.2 7.1 %collective-permute-start.16 = (f32[128,128]{1,0:T(8,128)S(1)}, f32[128,128]{1,0:T(8,128)S(1)}, u32[]{:S(2)}, u32[]{:S(2)}) collective-permute-start(f32[128,128]{1,0:T(8,128)S(1)} %get-tuple-element.164), channel_id=1, source_target_pairs={{0,33},{1,34},{2,35},{3,36},{4,37},{5,38},{6,39},{7,40},{8,41},{9,... | collective-permute-start | bytes 196616 | tf_op jit(solution)/shard_map/ppermute | solution.py:337
  162.1 6.3 %collective-permute-start.17 = (f32[128,128]{1,0:T(8,128)S(1)}, f32[128,128]{1,0:T(8,128)S(1)}, u32[]{:S(2)}, u32[]{:S(2)}) collective-permute-start(f32[128,128]{1,0:T(8,128)S(1)} %get-tuple-element.165), channel_id=1, source_target_pairs={{0,63},{1,32},{2,33},{3,34},{4,35},{5,36},{6,37},{7,38},{8,39},{9,... | collective-permute-start | bytes 196616 | tf_op jit(solution)/shard_map/ppermute | solution.py:337
  197.4 5.3 %collective-permute-start.18 = (f32[32,8,128]{2,1,0:T(8,128)S(1)}, f32[32,8,128]{2,1,0:T(8,128)S(1)}, u32[]{:S(2)}, u32[]{:S(2)}) collective-permute-start(f32[32,8,128]{2,1,0:T(8,128)S(1)} %all_to_all.43.refs_0_), channel_id=1, source_target_pairs={{0,32},{1,33},{2,34},{3,35},{4,36},{5,37},{6,38},{7,39},{8,40},{9,... | collective-permute-start | bytes 393224 | tf_op jit(solution)/shard_map/ppermute | solution.py:337
  206.0 10.4 %collective-permute-start.19 = (f32[128,1536]{1,0:T(8,128)S(1)}, f32[128,1536]{1,0:T(8,128)S(1)}, u32[]{:S(2)}, u32[]{:S(2)}) collective-permute-start(f32[128,1536]{1,0:T(8,128)S(1)} %get-tuple-element.181), channel_id=1, source_target_pairs={{0,32},{1,33},{2,34},{3,35},{4,36},{5,37},{6,38},{7,39},{8,40},{9,... | collective-permute-start | bytes 2359304 | tf_op jit(solution)/shard_map/ppermute | solution.py:337
  206.0 7.1 %collective-permute-start.20 = (f32[128,128]{1,0:T(8,128)S(1)}, f32[128,128]{1,0:T(8,128)S(1)}, u32[]{:S(2)}, u32[]{:S(2)}) collective-permute-start(f32[128,128]{1,0:T(8,128)S(1)} %get-tuple-element.182), channel_id=1, source_target_pairs={{0,33},{1,34},{2,35},{3,36},{4,37},{5,38},{6,39},{7,40},{8,41},{9,... | collective-permute-start | bytes 196616 | tf_op jit(solution)/shard_map/ppermute | solution.py:337
  206.1 7.0 %collective-permute-start.21 = (f32[128,128]{1,0:T(8,128)S(1)}, f32[128,128]{1,0:T(8,128)S(1)}, u32[]{:S(2)}, u32[]{:S(2)}) collective-permute-start(f32[128,128]{1,0:T(8,128)S(1)} %get-tuple-element.183), channel_id=1, source_target_pairs={{0,63},{1,32},{2,33},{3,34},{4,35},{5,36},{6,37},{7,38},{8,39},{9,... | collective-permute-start | bytes 196616 | tf_op jit(solution)/shard_map/ppermute | solution.py:337
  219.0 8.9 %collective-permute-start.22 = (f32[128,1536]{1,0:T(8,128)S(1)}, f32[128,1536]{1,0:T(8,128)S(1)}, u32[]{:S(2)}, u32[]{:S(2)}) collective-permute-start(f32[128,1536]{1,0:T(8,128)S(1)} %get-tuple-element.198.refs_8_), channel_id=1, source_target_pairs={{0,32},{1,33},{2,34},{3,35},{4,36},{5,37},{6,38},{7,39},{8,40},{9,... | collective-permute-start | bytes 2359304 | tf_op jit(solution)/shard_map/ppermute | solution.py:337
  222.7 7.1 %collective-permute-start.23 = (f32[128,128]{1,0:T(8,128)S(1)}, f32[128,128]{1,0:T(8,128)S(1)}, u32[]{:S(2)}, u32[]{:S(2)}) collective-permute-start(f32[128,128]{1,0:T(8,128)S(1)} %get-tuple-element.185), channel_id=1, source_target_pairs={{0,33},{1,34},{2,35},{3,36},{4,37},{5,38},{6,39},{7,40},{8,41},{9,... | collective-permute-start | bytes 196616 | tf_op jit(solution)/shard_map/ppermute | solution.py:337
  223.6 6.3 %collective-permute-start.24 = (f32[128,128]{1,0:T(8,128)S(1)}, f32[128,128]{1,0:T(8,128)S(1)}, u32[]{:S(2)}, u32[]{:S(2)}) collective-permute-start(f32[128,128]{1,0:T(8,128)S(1)} %get-tuple-element.186), channel_id=1, source_target_pairs={{0,63},{1,32},{2,33},{3,34},{4,35},{5,36},{6,37},{7,38},{8,39},{9,... | collective-permute-start | bytes 196616 | tf_op jit(solution)/shard_map/ppermute | solution.py:337
  259.0 5.3 %collective-permute-start.25 = (f32[32,8,128]{2,1,0:T(8,128)S(1)}, f32[32,8,128]{2,1,0:T(8,128)S(1)}, u32[]{:S(2)}, u32[]{:S(2)}) collective-permute-start(f32[32,8,128]{2,1,0:T(8,128)S(1)} %all_to_all.45.refs_0_), channel_id=1, source_target_pairs={{0,32},{1,33},{2,34},{3,35},{4,36},{5,37},{6,38},{7,39},{8,40},{9,... | collective-permute-start | bytes 393224 | tf_op jit(solution)/shard_map/ppermute | solution.py:337
